TPU v7x, 128 devices: a whole 4x4x4 slice. The times are simulated.
128 devices in a mesh: rep: 4 (over y), dev: 32 (over x, z, core).
Axes of the slice: x: 4, y: 4, z: 4, core: 2. Of those that a mesh axis runs over, the one named last changes fastest.
Arguments:
- queries: bfloat16 [256, 128, 576], P(('rep', 'dev')), parts along dimension 0, may hold values from -250 to 250
- latent_cache: bfloat16 [256, 1024, 576], P(('rep', 'dev')), parts along dimension 0, may hold values from -10 to 10
- lengths: int32 [256], P('rep'), parts along dimension 0, may hold values from 1 to 1024, 32768 in all
- trade_slot: int32 [64], P('rep'), parts along dimension 0, may hold values from 0 to 1
- tokens: bfloat16 [256, 3584], P(('rep', 'dev')), parts along dimension 0, may hold values from -6 to 6
- routing: int32 [256, 8], P(('rep', 'dev')), parts along dimension 0, may hold values from 0 to 31, all different within a row; in each aligned block of 2 rows (0 to 1, 2 to 3, ...) at most 2 rows name the same one
- gate_weights: float32 [256, 8], P(('rep', 'dev')), parts along dimension 0, may hold values from 0.05 to 0.5
- w_gate: bfloat16 [32, 3584, 1024], P('dev'), may hold values from -0.09375 to 0.09375
- w_up: bfloat16 [32, 3584, 1024], P('dev'), may hold values from -0.09375 to 0.09375
- w_down: bfloat16 [32, 1024, 3584], P('dev'), may hold values from -0.1875 to 0.1875
Outputs:
- attended: bfloat16 [256, 128, 512], P(('rep', 'dev')), parts along dimension 0
- expert_out: bfloat16 [256, 3584], P(('rep', 'dev')), parts along dimension 0
There are 4 independent parts, one for each index of `rep`. A program takes and returns all parts, laid end to end along the dimension named above; an argument that names none is the same for every part. Nothing has to cross between parts.
Inputs may be any that keep to these rules, and one draw needn't show every extreme that they name: `routing`: each token names 8 different experts; among the tokens of one device no expert is named more than 2 times.
All inputs are finite; a program needn't handle non-finite values.
Results may differ from a plain program's by a relative error of at most 0.011.
Values may be sent and summed in bfloat16 or wider, within the bound.
A program may use at most 128 MiB of HBM per device.

v0:
```python
from functools import partial

import jax
import jax.numpy as jnp
from jax import lax
from jax.sharding import PartitionSpec as P

LAT = 512


score_scale = 192.0 ** (-0.5)


def shifted(value, axis, steps):
    count = lax.axis_size(axis)
    pairs = [(source, (source + steps) % count) for source in range(count)]
    return lax.ppermute(value, axis, pairs)


def attend(queries, latents, live_len):
    scores = (
        jnp.einsum("rhc,rkc->rhk", queries, latents, preferred_element_type=jnp.float32)
        * score_scale
    )
    position = lax.broadcasted_iota(jnp.int32, scores.shape, 2)
    scores = jnp.where(position < live_len[:, None, None], scores, -jnp.inf)
    peak_score = jnp.max(scores, axis=2, keepdims=True)
    weights = jnp.exp(scores - peak_score)
    shares = (weights / jnp.sum(weights, axis=2, keepdims=True)).astype(jnp.bfloat16)
    return jnp.einsum(
        "rhk,rkc->rhc", shares, latents[:, :, :LAT], preferred_element_type=jnp.float32
    ).astype(jnp.bfloat16)


def run_experts(arrived, w_gate, w_up, w_down):
    gate = jnp.einsum("necd,edf->necf", arrived, w_gate, preferred_element_type=jnp.float32)
    upward = jnp.einsum("necd,edf->necf", arrived, w_up, preferred_element_type=jnp.float32)
    hidden = (jax.nn.silu(gate) * upward).astype(jnp.bfloat16)
    return jnp.einsum("necf,efd->necd", hidden, w_down, preferred_element_type=jnp.float32).astype(
        jnp.bfloat16
    )


def local(
    queries, latent_cache, lengths, trade_slot, tokens, routing, gate_weights, w_gate, w_up, w_down
):
    devices = lax.axis_size("dev")
    own_index = lax.axis_index("dev")
    half_way = devices // 2
    req_count = queries.shape[0]
    partner = (own_index + half_way) % devices
    trade_at = trade_slot[own_index % half_way]
    own_len = lax.dynamic_slice_in_dim(lengths, own_index * req_count, req_count)
    partner_len = lax.dynamic_slice_in_dim(lengths, partner * req_count, req_count)
    picked = lax.dynamic_slice_in_dim(latent_cache, trade_at, 1, 0)
    arrived_cache = shifted(picked, "dev", half_way)
    cache_now = lax.dynamic_update_slice_in_dim(latent_cache, arrived_cache, trade_at, 0)
    live_len = jnp.where(jnp.arange(req_count) == trade_at, partner_len, own_len)
    attended = attend(queries, cache_now, live_len)
    experts_dev = w_gate.shape[0]
    total_experts = experts_dev * devices
    tok_count = tokens.shape[0]
    top_count = routing.shape[1]
    capacity = max(2, 2 * (tok_count * top_count // total_experts))
    chosen = routing.reshape(-1)
    onehot = (chosen[:, None] == jnp.arange(total_experts, dtype=jnp.int32)[None, :]).astype(
        jnp.int32
    )
    earlier = jnp.cumsum(onehot, axis=0) - onehot
    position = jnp.sum(earlier * onehot, axis=1)
    target = chosen * capacity + position
    slot_ids = jnp.arange(total_experts * capacity, dtype=jnp.int32)
    placing = (slot_ids[:, None] == target[None, :]).astype(jnp.bfloat16)
    token_rows = jnp.take(
        tokens, jnp.arange(tok_count * top_count, dtype=jnp.int32) // top_count, axis=0
    )
    outgoing = jnp.dot(placing, token_rows, preferred_element_type=jnp.float32).astype(jnp.bfloat16)
    outgoing = outgoing.reshape(devices, experts_dev, capacity, tokens.shape[1])
    worker = partial(run_experts, w_gate=w_gate, w_up=w_up, w_down=w_down)
    produced = worker(lax.all_to_all(outgoing, "dev", split_axis=0, concat_axis=0, tiled=True))
    returned_rows = lax.all_to_all(produced, "dev", split_axis=0, concat_axis=0, tiled=True)
    flat_rows = returned_rows.reshape(devices * experts_dev * capacity, tokens.shape[1])
    taken = jnp.take(flat_rows, target, axis=0).astype(jnp.float32)
    weighted = taken * gate_weights.reshape(-1)[:, None]
    expert_out = jnp.sum(weighted.reshape(tok_count, top_count, tokens.shape[1]), axis=1).astype(
        jnp.bfloat16
    )
    return (attended, expert_out)


def solution(mesh):
    in_specs = (
        P(("rep", "dev"), None, None),
        P(("rep", "dev"), None, None),
        P("rep"),
        P("rep"),
        P(("rep", "dev"), None),
        P(("rep", "dev"), None),
        P(("rep", "dev"), None),
        P("dev", None, None),
        P("dev", None, None),
        P("dev", None, None),
    )
    out_specs = (P(("rep", "dev"), None, None), P(("rep", "dev"), None))
    return jax.shard_map(local, mesh=mesh, in_specs=in_specs, out_specs=out_specs, check_vma=False)
```

profile of v0, /device:TPU:1, one launch (start us, length us, event | category | flops | bytes accessed | tf_op | source)
XLA Modules:
  0.0 86.7 jit_solution(8689532228550368232)
XLA Ops:
  0.6 0.0 copy-start
  0.6 0.0 copy-start.1
  0.7 1.3 %dynamic_slice.12 = s32[1]{0:T(128)} dynamic-slice(s32[16]{0:T(128)} %param.13, s32[]{:T(128)S(6)} %select_n.89), dynamic_slice_sizes={1} | dynamic-slice | bytes 12 | tf_op jit(solution)/shard_map/dynamic_slice | solution.py:52
  3.9 0.0 copy-start.2
  3.9 2.5 %constant_dynamic-slice_fusion = bf16[1,1024,576]{1,2,0:T(8,128)(2,1)} fusion(bf16[2,1024,576]{1,2,0:T(8,128)(2,1)} %param.11, s32[]{:T(128)S(6)} %select_n.94), kind=kLoop, calls=%fused_computation.71 | loop fusion | bytes 2359300 | tf_op jit(solution)/shard_map/dynamic_slice | solution.py:55
  6.4 3.6 %collective-permute-start = (bf16[1,1024,576]{1,2,0:T(8,128)(2,1)}, bf16[1,1024,576]{1,2,0:T(8,128)(2,1)}, u32[]{:S(2)}, u32[]{:S(2)}) collective-permute-start(bf16[1,1024,576]{1,2,0:T(8,128)(2,1)} %constant_dynamic-slice_fusion), channel_id=1, source_target_pairs={{0,16},{1,17},{2,18},{3,19},{4,20},{5,21},{6,22},{7,23},{8,24},{9,... | collective-permute-start | bytes 3538952 | tf_op jit(solution)/shard_map/ppermute | solution.py:17
  10.0 0.8 reshape.141
  10.8 0.1 fusion.56
  10.9 0.2 select_reduce_fusion
  11.1 0.0 copy-done.1
  11.1 0.6 gather_fusion
  11.7 0.3 convolution_convert_fusion
  12.1 0.9 %reshape.142 = bf16[32,1,2,3584]{3,2,0,1:T(2,128)(2,1)} reshape(bf16[64,3584]{1,0:T(8,128)(2,1)S(1)} %convolution_convert_fusion) | data formatting | bytes 917504 | tf_op jit(solution)/shard_map/reshape | solution.py:78
  13.0 7.0 %all-to-all-start = ((bf16[32,1,2,3584]{3,2,1,0:T(2,128)(2,1)}), bf16[32,1,2,3584]{3,2,1,0:T(2,128)(2,1)S(1)}, u32[]{:S(2)}, u32[]{:S(2)}) async-start(bf16[32,1,2,3584]{3,2,1,0:T(2,128)(2,1)} %bitcast.86), calls=%async_computation | async-start | bytes 917504 | tf_op jit(solution)/shard_map/all_to_all | solution.py:80
  20.0 0.0 copy-done.2
  20.0 0.0 copy-start.5
  20.0 2.6 %copy.23 = bf16[2,1024,576]{2,1,0:T(8,128)(2,1)} copy(bf16[2,1024,576]{1,2,0:T(8,128)(2,1)S(1)} %copy-done.2) | data formatting | bytes 4718592 | tf_op args[1]
  22.6 0.1 reduce_sum.33
  22.7 0.0 copy-done.5
  22.7 0.1 mul.66
  22.8 22.3 %all-to-all-done = bf16[32,1,2,3584]{3,2,1,0:T(2,128)(2,1)S(1)} async-done(((bf16[32,1,2,3584]{3,2,1,0:T(2,128)(2,1)}), bf16[32,1,2,3584]{3,2,1,0:T(2,128)(2,1)S(1)}, u32[]{:S(2)}, u32[]{:S(2)}) %all-to-all-start) | async-done | bytes 458784 | tf_op jit(solution)/shard_map/all_to_all | solution.py:80
  45.1 4.5 %fusion.22 = f32[32,1,2,1024]{3,0,2,1:T(8,128)S(1)} fusion(bf16[1,3584,1024]{2,1,0:T(8,128)(2,1)} %param.17, bf16[32,1,2,3584]{3,2,1,0:T(2,128)(2,1)S(1)} %all-to-all-done), kind=kOutput, calls=%fused_computation.20 | convolution fusion | flops 469762048 | bytes 8060928 | tf_op jit(solution)/shard_map/necd,edf->necf/dot_general | solution.py:36
  49.6 0.0 copy-start.6
  49.6 7.9 %fusion.10 = bf16[32,1,2,3584]{3,0,2,1:T(8,128)(2,1)S(1)} fusion(bf16[1,1024,3584]{2,1,0:T(8,128)(2,1)} %param.19, bf16[1,3584,1024]{2,1,0:T(8,128)(2,1)} %param.18, bf16[32,1,2,3584]{3,2,1,0:T(2,128)(2,1)S(1)} %all-to-all-done, f32[32,1,2,1024]{3,0,2,1:T(8,128)S(1)} %fusion.22), kind=kOutput, calls=%fused_computation.11 | convolution fusion | flops 940146688 | bytes 15859712 | tf_op jit(solution)/shard_map/necf,efd->necd/dot_general | solution.py:39
  57.5 0.0 copy-start.7
  57.5 1.2 %copy.29 = bf16[32,1,2,3584]{3,2,1,0:T(2,128)(2,1)} copy(bf16[32,1,2,3584]{3,0,2,1:T(8,128)(2,1)S(1)} %fusion.10) | data formatting | bytes 917504 | tf_op jit(solution)/shard_map/convert_element_type | solution.py:39
  58.7 5.5 %all-to-all-start.1 = ((bf16[32,1,2,3584]{3,2,1,0:T(2,128)(2,1)}), bf16[32,1,2,3584]{3,2,1,0:T(2,128)(2,1)S(1)}, u32[]{:S(2)}, u32[]{:S(2)}) async-start(bf16[32,1,2,3584]{3,2,1,0:T(2,128)(2,1)} %copy.29), calls=%async_computation.1 | async-start | bytes 917504 | tf_op jit(solution)/shard_map/all_to_all | solution.py:81
  64.3 0.0 copy-done.6
  64.3 0.7 compare_select_fusion.4
  65.0 10.2 %all-to-all-done.1 = bf16[32,1,2,3584]{3,2,1,0:T(2,128)(2,1)S(1)} async-done(((bf16[32,1,2,3584]{3,2,1,0:T(2,128)(2,1)}), bf16[32,1,2,3584]{3,2,1,0:T(2,128)(2,1)S(1)}, u32[]{:S(2)}, u32[]{:S(2)}) %all-to-all-start.1) | async-done | bytes 458784 | tf_op jit(solution)/shard_map/all_to_all | solution.py:81
  75.2 0.2 reshape.148
  75.4 0.6 gather_fusion.1
  76.0 0.0 copy-done.7
  76.0 0.8 multiply_reduce_fusion
  76.8 0.0 collective-permute-done
  76.8 1.7 %copy.24 = bf16[1,1024,576]{2,1,0:T(8,128)(2,1)S(1)} copy(bf16[1,1024,576]{1,2,0:T(8,128)(2,1)} %collective-permute-done) | data formatting | bytes 2359296 | tf_op jit(solution)/shard_map/ppermute | solution.py:17
  78.5 1.2 %constant_dynamic-update-slice_fusion = bf16[2,1024,576]{2,1,0:T(8,128)(2,1)} fusion(bf16[2,1024,576]{2,1,0:T(8,128)(2,1)} %copy.23, bf16[1,1024,576]{2,1,0:T(8,128)(2,1)S(1)} %copy.24, s32[]{:T(128)S(6)} %select_n.94), kind=kLoop, calls=%fused_computation.70 | loop fusion | bytes 2490372 | tf_op jit(solution)/shard_map/dynamic_update_slice | solution.py:57
  79.7 0.0 copy-done
  79.7 0.0 copy-start.3
  79.7 2.8 %fusion.18 = f32[2,128,1024]{1,2,0:T(8,128)S(1)} fusion(bf16[2,1024,576]{2,1,0:T(8,128)(2,1)} %constant_dynamic-update-slice_fusion, bf16[2,128,576]{1,2,0:T(8,128)(2,1)S(1)} %copy-done, s32[2]{0:T(128)S(1)} %compare_select_fusion.4), kind=kOutput, calls=%fused_computation.18 | convolution fusion | flops 302776320 | bytes 3702792 | tf_op jit(solution)/shard_map/rhc,rkc->rhk/dot_general | solution.py:22
  82.4 0.0 copy-start.4
  82.4 1.0 %copy-done.4 = f32[2,128,1024]{1,2,0:T(8,128)} copy-done((f32[2,128,1024]{1,2,0:T(8,128)}, f32[2,128,1024]{1,2,0:T(8,128)S(1)}, u32[]{:S(2)}) %copy-start.4) | copy-done | bytes 1048600
  83.4 0.4 fusion.62
  83.8 0.0 copy-done.3
  83.8 2.9 %fusion.19 = bf16[2,128,512]{2,1,0:T(8,128)(2,1)} fusion(bf16[2,1024,576]{2,1,0:T(8,128)(2,1)S(1)} %copy-done.3, f32[2,128]{1,0:T(2,128)S(1)} %fusion.62, f32[2,128,1024]{1,2,0:T(8,128)} %copy-done.4), kind=kOutput, calls=%fused_computation.19 | convolution fusion | flops 269354240 | bytes 4457472 | tf_op jit(solution)/shard_map/rhk,rkc->rhc/dot_general | solution.py:30
  (9 shorter events, 0.1 us)
Async XLA Ops:
  0.6 79.0 %copy-start = (bf16[2,128,576]{1,2,0:T(8,128)(2,1)S(1)}, bf16[2,128,576]{1,2,0:T(8,128)(2,1)}, u32[]{:S(2)}) copy-start(bf16[2,128,576]{1,2,0:T(8,128)(2,1)} %param.10) | copy-start | bytes 884740
  0.6 10.5 %copy-start.1 = (bf16[2,3584]{1,0:T(2,128)(2,1)S(1)}, bf16[2,3584]{1,0:T(2,128)(2,1)}, u32[]{:S(2)}) copy-start(bf16[2,3584]{1,0:T(2,128)(2,1)} %param.14) | copy-start | bytes 43012
  3.9 16.1 %copy-start.2 = (bf16[2,1024,576]{1,2,0:T(8,128)(2,1)S(1)}, bf16[2,1024,576]{1,2,0:T(8,128)(2,1)}, u32[]{:S(2)}) copy-start(bf16[2,1024,576]{1,2,0:T(8,128)(2,1)} %param.11) | copy-start | bytes 7077892
  6.4 70.3 %collective-permute-start = (bf16[1,1024,576]{1,2,0:T(8,128)(2,1)}, bf16[1,1024,576]{1,2,0:T(8,128)(2,1)}, u32[]{:S(2)}, u32[]{:S(2)}) collective-permute-start(bf16[1,1024,576]{1,2,0:T(8,128)(2,1)} %constant_dynamic-slice_fusion), channel_id=1, source_target_pairs={{0,16},{1,17},{2,18},{3,19},{4,20},{5,21},{6,22},{7,23},{8,24},{9,... | collective-permute-start | bytes 3538952 | tf_op jit(solution)/shard_map/ppermute | solution.py:17
  13.0 32.1 %all-to-all-start = ((bf16[32,1,2,3584]{3,2,1,0:T(2,128)(2,1)}), bf16[32,1,2,3584]{3,2,1,0:T(2,128)(2,1)S(1)}, u32[]{:S(2)}, u32[]{:S(2)}) async-start(bf16[32,1,2,3584]{3,2,1,0:T(2,128)(2,1)} %bitcast.86), calls=%async_computation | async-start | bytes 917504 | tf_op jit(solution)/shard_map/all_to_all | solution.py:80
  20.0 2.7 %copy-start.5 = (s32[2,8]{1,0:T(2,128)S(1)}, s32[2,8]{1,0:T(2,128)}, u32[]{:S(2)}) copy-start(s32[2,8]{1,0:T(2,128)} %param.15) | copy-start | bytes 196
  49.6 14.6 %copy-start.6 = (s32[64]{0:T(128)S(1)}, s32[64]{0:T(128)}, u32[]{:S(2)}) copy-start(s32[64]{0:T(128)} %param.12) | copy-start | bytes 772
  57.5 18.5 %copy-start.7 = (f32[2,8]{1,0:T(2,128)S(1)}, f32[2,8]{1,0:T(2,128)}, u32[]{:S(2)}) copy-start(f32[2,8]{1,0:T(2,128)} %param.16) | copy-start | bytes 196
  58.7 16.5 %all-to-all-start.1 = ((bf16[32,1,2,3584]{3,2,1,0:T(2,128)(2,1)}), bf16[32,1,2,3584]{3,2,1,0:T(2,128)(2,1)S(1)}, u32[]{:S(2)}, u32[]{:S(2)}) async-start(bf16[32,1,2,3584]{3,2,1,0:T(2,128)(2,1)} %copy.29), calls=%async_computation.1 | async-start | bytes 917504 | tf_op jit(solution)/shard_map/all_to_all | solution.py:81
  79.7 4.1 %copy-start.3 = (bf16[2,1024,576]{2,1,0:T(8,128)(2,1)S(1)}, bf16[2,1024,576]{2,1,0:T(8,128)(2,1)}, u32[]{:S(2)}) copy-start(bf16[2,1024,576]{2,1,0:T(8,128)(2,1)} %constant_dynamic-update-slice_fusion) | copy-start | bytes 7077892
  82.4 1.0 %copy-start.4 = (f32[2,128,1024]{1,2,0:T(8,128)}, f32[2,128,1024]{1,2,0:T(8,128)S(1)}, u32[]{:S(2)}) copy-start(f32[2,128,1024]{1,2,0:T(8,128)S(1)} %fusion.18) | copy-start | bytes 3145732
where the time goes:
time: 87.2 us; the launch traced here: 86.7 us
  waiting for transfers between devices  32.6 us (37%)
  matrix products  18.3 us (21%)
  starting transfers between devices  16.1 us (18%)
  local copies, waits for them, and re-layouts  14.8 us (17%)
  between operations  2.77 us (3%)
  other arithmetic  2.18 us (3%)
    all_to_all x1, waiting for transfers between devices, local(): lax.all_to_all(outgoing, 'dev', split_axis=0, concat_axis=0, tiled=True)  22.3 us
    all_to_all x1, waiting for transfers between devices, local(): lax.all_to_all(produced, 'dev', split_axis=0, concat_axis=0, tiled=True)  10.2 us
    dot_general x1, matrix products, run_experts(): jnp.einsum('necf,efd->necd', hidden, w_down, preferred_element_type=jnp.f...  7.86 us
    all_to_all x1, starting transfers between devices, local(): lax.all_to_all(outgoing, 'dev', split_axis=0, concat_axis=0, tiled=True)  7 us
    all_to_all x1, starting transfers between devices, local(): lax.all_to_all(produced, 'dev', split_axis=0, concat_axis=0, tiled=True)  5.5 us
    dot_general x1, matrix products, run_experts(): jnp.einsum('necd,edf->necf', arrived, w_gate, preferred_element_type=jnp....  4.46 us
    unnamed x17, local copies, waits for them, and re-layouts  3.61 us
    ppermute x1, starting transfers between devices, shifted(): return lax.ppermute(value, axis, pairs)  3.57 us
  transfers between devices with their start and end apart: 3, of which 2 were waited for; matrix products, arithmetic and copies ran while one was open for 25% of the time, Pallas kernels for 0%

commit v1 on v0

v1 whole, which is shorter than its diff:
```python
import functools

import jax
import jax.numpy as jnp
from jax import lax
from jax.experimental import pallas as pl
from jax.experimental.pallas import tpu as pltpu
from jax.sharding import PartitionSpec as P

LAT = 512
W = 512
PIECES = 7
SLOTS = 8
score_scale = 192.0 ** (-0.5)
MESH = pl.DeviceIdType.MESH
f32 = jnp.float32
bf16 = jnp.bfloat16


def send(src, dst, send_sem, recv_sem, to):
    return pltpu.make_async_remote_copy(
        src_ref=src,
        dst_ref=dst,
        send_sem=send_sem,
        recv_sem=recv_sem,
        device_id={"dev": to},
        device_id_type=MESH,
    )


def attend(q_t, k_t, live):
    scores = (
        lax.dot_general(q_t, k_t, (((0,), (0,)), ((), ())), preferred_element_type=f32)
        * score_scale
    )
    position = lax.broadcasted_iota(jnp.int32, scores.shape, 1)
    scores = jnp.where(position < live, scores, -jnp.inf)
    weights = jnp.exp(scores - jnp.max(scores, axis=1, keepdims=True))
    shares = (weights / jnp.sum(weights, axis=1, keepdims=True)).astype(bf16)
    return lax.dot_general(
        shares, k_t[:LAT], (((1,), (1,)), ((), ())), preferred_element_type=f32
    ).astype(bf16)


def kernel(
    q_hbm, k_hbm, lengths, trade_slot, tok_hbm, rout_hbm, gw_hbm, wg_hbm, wu_hbm, wd_hbm,
    att_hbm, exp_ref,
    tok, rout, gw, q, k, wg, wu, wd, stage, perm, gathered, q_out, q_in, o_out, o_in, att,
    sums, mate_in, back, landed,
    small_sem, q_sem, k_sem, wg_sem, wu_sem, wd_sem, att_sem,
    tok_s, tok_r, fwd_s, fwd_r, trade_s, trade_r, mate_s, mate_r, back_s, back_r,
):
    me = lax.axis_index("dev")
    chip, core = me // 2, me % 2
    cx, cz = chip // 4, chip % 4
    mate = chip * 2 + (1 - core)
    partner = (me + 16) % 32
    away = [(dx, dz) for dx in (2, 1, 3, 0) for dz in (2, 1, 3, 0) if (dx, dz) != (0, 0)]
    to_chip = [((cx + dx) % 4) * 4 + (cz + dz) % 4 for dx, dz in away]
    from_chip = [((cx + 4 - dx) % 4) * 4 + (cz + 4 - dz) % 4 for dx, dz in away]

    barrier = pltpu.get_barrier_semaphore()
    for other in [c * 2 + core for c in to_chip] + [mate]:
        pl.semaphore_signal(barrier, inc=1, device_id={"dev": other}, device_id_type=MESH)

    loads = [
        pltpu.make_async_copy(tok_hbm, tok, small_sem.at[0]),
        pltpu.make_async_copy(rout_hbm, rout, small_sem.at[1]),
        pltpu.make_async_copy(gw_hbm, gw, small_sem.at[2]),
        pltpu.make_async_copy(q_hbm, q, q_sem),
        pltpu.make_async_copy(k_hbm, k, k_sem),
    ]
    tok_load, rout_load, gw_load, q_load, k_load = loads
    wg_loads, wu_loads, wd_loads = [], [], []
    for s in range(PIECES):
        rows = pl.ds(s * W, W)
        wg_loads.append(pltpu.make_async_copy(wg_hbm.at[0, rows], wg.at[rows], wg_sem.at[s]))
        wu_loads.append(pltpu.make_async_copy(wu_hbm.at[0, rows], wu.at[rows], wu_sem.at[s]))
        wd_loads.append(
            pltpu.make_async_copy(wd_hbm.at[0, :, rows], wd.at[:, rows], wd_sem.at[s])
        )
    for load in loads:
        load.start()
    for s in range(PIECES):
        wg_loads[s].start()
        wu_loads[s].start()
    for s in range(PIECES):
        wd_loads[s].start()

    tok_load.wait()
    rout_load.wait()
    gw_load.wait()
    tokens = tok[...].astype(f32)
    lane = lax.broadcasted_iota(jnp.int32, (2, W), 1)
    factor = jnp.zeros((2, W), f32)
    for top in range(8):
        expert, weight = rout[:, top : top + 1], gw[:, top : top + 1]
        hit = (lane == expert) | (lane == expert + 32)
        factor = factor + jnp.where(hit, weight, 0.0)
    high = factor.astype(bf16).astype(f32)
    factor = jnp.where(lane < 32, high, factor - high)
    for t in range(2):
        for s in range(PIECES):
            stage[t * SLOTS + s : t * SLOTS + s + 1, :] = tokens[t : t + 1, s * W : (s + 1) * W]
        stage[t * SLOTS + PIECES : (t + 1) * SLOTS, :] = factor[t : t + 1]
    gathered[core, chip] = stage[...].astype(bf16)

    pl.semaphore_wait(barrier, 16)

    own = gathered.at[core, chip]
    tok_copies = [
        send(own, own, tok_s.at[i], tok_r.at[i], to_chip[i] * 2 + core) for i in range(15)
    ]
    own_copy = send(own, own, fwd_s.at[15], fwd_r.at[15], mate)
    for copy in tok_copies:
        copy.start()
    own_copy.start()

    trade_at = trade_slot[me % 16]
    keep_at = 1 - trade_at
    q_load.wait()
    q_out[...] = q[trade_at]
    q_copy = send(q_out, q_in, trade_s.at[0], trade_r.at[0], partner)
    q_copy.start()

    row = lax.broadcasted_iota(jnp.int32, (512, 512), 0)
    col = lax.broadcasted_iota(jnp.int32, (512, 512), 1)
    perm[...] = jnp.where(col == (row % 64) * SLOTS + row // 64, 1.0, 0.0).astype(bf16)

    k_load.wait()
    kept = attend(q[keep_at], k[keep_at], lengths[me * 2 + keep_at])

    fwd_copies = []
    for i in range(15):
        tok_copies[i].wait_recv()
        block = gathered.at[core, from_chip[i]]
        fwd_copies.append(send(block, block, fwd_s.at[i], fwd_r.at[i], mate))
        fwd_copies[i].start()

    q_copy.wait_recv()
    o_out[...] = attend(q_in[...], k[trade_at], lengths[me * 2 + trade_at])
    o_copy = send(o_out, o_in, trade_s.at[1], trade_r.at[1], partner)
    o_copy.start()

    for copy in fwd_copies + [own_copy]:
        copy.wait_recv()
    rows = gathered[...].reshape(512, W)

    gate = jnp.zeros((64, 1024), f32)
    up = jnp.zeros((64, 1024), f32)
    for s in range(PIECES):
        x = jnp.dot(perm[s * 64 : (s + 1) * 64, :], rows, preferred_element_type=f32).astype(bf16)
        wg_loads[s].wait()
        gate += jnp.dot(x, wg[s * W : (s + 1) * W, :], preferred_element_type=f32)
        wu_loads[s].wait()
        up += jnp.dot(x, wu[s * W : (s + 1) * W, :], preferred_element_type=f32)
    factors = jnp.dot(perm[PIECES * 64 :, :], rows, preferred_element_type=f32)
    lane = lax.broadcasted_iota(jnp.int32, (64, W), 1)
    mine = (lane == me) | (lane == me + 32)
    weight = jnp.sum(jnp.where(mine, factors, 0.0), axis=1, keepdims=True)
    hidden = (gate / (1.0 + jnp.exp(-gate)) * up).astype(bf16)

    mate_copies = []
    for s in range(PIECES):
        wd_loads[s].wait()
        y = jnp.dot(hidden, wd[:, s * W : (s + 1) * W], preferred_element_type=f32).astype(bf16)
        sums[s] = (y.astype(f32) * weight).astype(bf16).reshape(2, 32, W)
        mate_copies.append(
            send(sums.at[s, 1 - core], mate_in.at[s], mate_s.at[s], mate_r.at[s], mate)
        )
        mate_copies[s].start()
    parts = []
    for s in range(PIECES):
        mate_copies[s].wait_recv()
        parts.append((sums[s, core].astype(f32) + mate_in[s].astype(f32)).astype(bf16))
    parts.append(jnp.zeros((32, W), bf16))
    row = lax.broadcasted_iota(jnp.int32, (256, 256), 0)
    col = lax.broadcasted_iota(jnp.int32, (256, 256), 1)
    unperm = jnp.where(col == (row % SLOTS) * 32 + row // SLOTS, 1.0, 0.0).astype(bf16)
    back[...] = (
        jnp.dot(unperm, jnp.concatenate(parts, axis=0), preferred_element_type=f32)
        .astype(bf16)
        .reshape(16, 16, W)
    )
    back_copies = [
        send(
            back.at[to_chip[i]], landed.at[chip], back_s.at[i], back_r.at[i], to_chip[i] * 2 + core
        )
        for i in range(15)
    ]
    for copy in back_copies:
        copy.start()
    landed[chip] = back[chip]

    o_copy.wait_recv()
    arrived = o_in[...]
    att[0] = jnp.where(trade_at == 0, arrived, kept)
    att[1] = jnp.where(trade_at == 1, arrived, kept)
    att_copy = pltpu.make_async_copy(att, att_hbm, att_sem)
    att_copy.start()

    for copy in back_copies:
        copy.wait_recv()
    total = landed[0].astype(f32)
    for c in range(1, 16):
        total += landed[c].astype(f32)
    exp_ref[...] = total.astype(bf16)

    att_copy.wait()
    for copy in tok_copies + fwd_copies + mate_copies + back_copies + [own_copy, q_copy, o_copy]:
        copy.wait_send()


def local(
    queries, latent_cache, lengths, trade_slot, tokens, routing, gate_weights, w_gate, w_up, w_down
):
    any_spec = pl.BlockSpec(memory_space=pl.ANY)
    smem_spec = pl.BlockSpec(memory_space=pltpu.SMEM)
    dma = pltpu.SemaphoreType.DMA
    vmem = pltpu.VMEM
    attended, rows = pl.pallas_call(
        kernel,
        out_shape=(
            jax.ShapeDtypeStruct((2, 128, LAT), bf16),
            jax.ShapeDtypeStruct((16, W), bf16),
        ),
        in_specs=[any_spec, any_spec, smem_spec, smem_spec] + [any_spec] * 6,
        out_specs=(any_spec, pl.BlockSpec(memory_space=pltpu.VMEM)),
        scratch_shapes=[
            vmem((2, 3584), bf16),
            vmem((2, 8), jnp.int32),
            vmem((2, 8), f32),
            vmem((2, 576, 128), bf16),
            vmem((2, 576, 1024), bf16),
            vmem((3584, 1024), bf16),
            vmem((3584, 1024), bf16),
            vmem((1024, 3584), bf16),
            vmem((16, W), f32),
            vmem((512, 512), bf16),
            vmem((2, 16, 16, W), bf16),
            vmem((576, 128), bf16),
            vmem((576, 128), bf16),
            vmem((128, LAT), bf16),
            vmem((128, LAT), bf16),
            vmem((2, 128, LAT), bf16),
            vmem((PIECES, 2, 32, W), bf16),
            vmem((PIECES, 32, W), bf16),
            vmem((16, 16, W), bf16),
            vmem((16, 16, W), bf16),
            dma((3,)),
            dma,
            dma,
            dma((PIECES,)),
            dma((PIECES,)),
            dma((PIECES,)),
            dma,
            dma((15,)),
            dma((15,)),
            dma((16,)),
            dma((16,)),
            dma((2,)),
            dma((2,)),
            dma((PIECES,)),
            dma((PIECES,)),
            dma((15,)),
            dma((15,)),
        ],
        compiler_params=pltpu.CompilerParams(
            collective_id=0, has_side_effects=True, vmem_limit_bytes=50 * 2**20
        ),
        cost_estimate=pl.CostEstimate(
            flops=2_000_000_000, bytes_accessed=25_000_000, transcendentals=400_000
        ),
    )(
        jnp.swapaxes(queries, 1, 2),
        jnp.swapaxes(latent_cache, 1, 2),
        lengths,
        trade_slot,
        tokens,
        routing,
        gate_weights,
        w_gate,
        w_up,
        w_down,
    )
    expert_out = rows.reshape(2, SLOTS, W)[:, :PIECES].reshape(2, PIECES * W)
    return attended, expert_out


def solution(mesh):
    in_specs = (
        P(("rep", "dev"), None, None),
        P(("rep", "dev"), None, None),
        P("rep"),
        P("rep"),
        P(("rep", "dev"), None),
        P(("rep", "dev"), None),
        P(("rep", "dev"), None),
        P("dev", None, None),
        P("dev", None, None),
        P("dev", None, None),
    )
    out_specs = (P(("rep", "dev"), None, None), P(("rep", "dev"), None))
    return jax.shard_map(local, mesh=mesh, in_specs=in_specs, out_specs=out_specs, check_vma=False)
```

time: 87.2 us -> 39.7 us (0.46)
  waiting for transfers between devices: 32.6 us -> 0 us
  Pallas kernels: 0 us -> 31.5 us
  matrix products: 18.3 us -> 0 us
  starting transfers between devices: 16.1 us -> 0 us
  local copies, waits for them, and re-layouts: 14.8 us -> 7.31 us
  other arithmetic: 2.18 us -> 0 us
  between operations: 2.77 us -> 0.66 us
    all_to_all x2 -> x0, waiting for transfers between devices: 32.6 us -> none  [the longest x1 22.3 us: local(): lax.all_to_all(outgoing, 'dev', split_axis=0, concat_axis=0, tiled=True)]
    pallas_call x0 -> x1, Pallas kernels: none -> 31.5 us  [local(): pl.pallas_call(kernel, out_shape=(jax.ShapeDtypeStruct((2, 128, LAT), bf1...]
    dot_general x5 -> x0, matrix products: 18.3 us -> none  [the longest x1 7.86 us: run_experts(): jnp.einsum('necf,efd->necd', hidden, w_down, preferred_element_type=jnp.f...]
    all_to_all x2 -> x0, starting transfers between devices: 12.5 us -> none  [the longest x1 7 us: local(): lax.all_to_all(outgoing, 'dev', split_axis=0, concat_axis=0, tiled=True)]
    dynamic_slice x2 -> x0, local copies, waits for them, and re-layouts: 3.81 us -> none  [the longest x1 2.53 us: local(): picked = lax.dynamic_slice_in_dim(latent_cache, trade_at, 1, 0)]
    unnamed x17, local copies, waits for them, and re-layouts: 3.61 us -> 7.31 us
    ppermute x1 -> x0, starting transfers between devices: 3.57 us -> none  [shifted(): return lax.ppermute(value, axis, pairs)]
    reshape x3 -> x0, local copies, waits for them, and re-layouts: 1.87 us -> none  [the longest x1 0.94 us: local(): outgoing = outgoing.reshape(devices, experts_dev, capacity, tokens.shape[1])]
  transfers between devices with their start and end apart: 3 -> 0, of which waited for: 2 -> 0; matrix products, arithmetic and copies ran while one was open for 25% -> 0% of each run, Pallas kernels for 0% -> 0%
where the time goes in v1:
time: 39.7 us; the launch traced here: 39.5 us
  Pallas kernels  31.5 us (79%)
  local copies, waits for them, and re-layouts  7.31 us (18%)
  between operations  0.66 us (2%)
    pallas_call x1, Pallas kernels, local(): pl.pallas_call(kernel, out_shape=(jax.ShapeDtypeStruct((2, 128, LAT), bf1...  31.5 us
    unnamed x17, local copies, waits for them, and re-layouts  7.31 us

profile of v1, /device:TPU:1, one launch (start us, length us, event | category | flops | bytes accessed | tf_op | source)
XLA Modules:
  0.0 39.5 jit_solution(10794614489360451816)
XLA Ops:
  0.6 0.0 copy-start
  0.6 1.7 %copy-done = bf16[2,1024,576]{1,2,0:T(8,128)(2,1)S(1)} copy-done((bf16[2,1024,576]{1,2,0:T(8,128)(2,1)S(1)}, bf16[2,1024,576]{1,2,0:T(8,128)(2,1)}, u32[]{:S(2)}) %copy-start) | copy-done | bytes 2359320
  2.3 0.0 copy-start.1
  2.3 1.0 %copy-done.1 = bf16[2,128,576]{1,2,0:T(8,128)(2,1)S(1)} copy-done((bf16[2,128,576]{1,2,0:T(8,128)(2,1)S(1)}, bf16[2,128,576]{1,2,0:T(8,128)(2,1)}, u32[]{:S(2)}) %copy-start.1) | copy-done | bytes 294936
  3.3 0.0 copy-start.2
  3.3 0.7 %copy-done.2 = bf16[2,3584]{1,0:T(2,128)(2,1)S(1)} copy-done((bf16[2,3584]{1,0:T(2,128)(2,1)S(1)}, bf16[2,3584]{1,0:T(2,128)(2,1)}, u32[]{:S(2)}) %copy-start.2) | copy-done | bytes 14360
  4.0 0.0 copy-start.3
  4.0 0.7 %copy-done.3 = s32[2,8]{1,0:T(2,128)S(1)} copy-done((s32[2,8]{1,0:T(2,128)S(1)}, s32[2,8]{1,0:T(2,128)}, u32[]{:S(2)}) %copy-start.3) | copy-done | bytes 88
  4.7 0.0 copy-start.4
  4.7 0.7 %copy-done.4 = f32[2,8]{1,0:T(2,128)S(1)} copy-done((f32[2,8]{1,0:T(2,128)S(1)}, f32[2,8]{1,0:T(2,128)}, u32[]{:S(2)}) %copy-start.4) | copy-done | bytes 88
  5.3 0.0 copy-start.5
  5.3 0.7 %copy-done.5 = s32[64]{0:T(128)S(1)} copy-done((s32[64]{0:T(128)S(1)}, s32[64]{0:T(128)}, u32[]{:S(2)}) %copy-start.5) | copy-done | bytes 280
  6.0 0.0 copy-start.6
  6.0 0.7 %copy-done.6 = s32[16]{0:T(128)S(1)} copy-done((s32[16]{0:T(128)S(1)}, s32[16]{0:T(128)}, u32[]{:S(2)}) %copy-start.6) | copy-done | bytes 88
  6.6 31.5 %shard_map.113 = (bf16[2,128,512]{2,1,0:T(8,128)(2,1)S(1)}, bf16[16,512]{1,0:T(8,128)(2,1)S(1)}) custom-call(bf16[2,576,128]{2,1,0:T(8,128)(2,1)S(1)} %bitcast.7, bf16[2,576,1024]{2,1,0:T(8,128)(2,1)S(1)} %bitcast.6, s32[64]{0:T(128)S(1)} %copy-done.5, s32[16]{0:T(128)S(1)} %copy-done.6, bf16[2,3584]{1,0:T(2,128)(2,1)S(1)} %copy-done.2, ...), custom_call_target="tpu_custom_call" | custom-call | flops 2000000000 | bytes 25000000 | tf_op jit(solution)/shard_map/pallas_call | solution.py:221
  38.1 0.6 %copy.12 = bf16[1,2,7,512]{3,1,2,0:T(2,128)(2,1)} copy(bf16[1,2,7,512]{3,2,1,0:T(8,128)(2,1)S(1)} %slice_bitcast_fusion) | data formatting | bytes 28672
  38.7 0.7 %copy.14 = bf16[2,128,512]{2,1,0:T(8,128)(2,1)} copy(bf16[2,128,512]{2,1,0:T(8,128)(2,1)S(1)} %get-tuple-element.8) | data formatting | bytes 524288
  (1 shorter events, 0.0 us)
Async XLA Ops:
  0.6 1.7 %copy-start = (bf16[2,1024,576]{1,2,0:T(8,128)(2,1)S(1)}, bf16[2,1024,576]{1,2,0:T(8,128)(2,1)}, u32[]{:S(2)}) copy-start(bf16[2,1024,576]{1,2,0:T(8,128)(2,1)} %param.11) | copy-start | bytes 7077892
  2.3 1.0 %copy-start.1 = (bf16[2,128,576]{1,2,0:T(8,128)(2,1)S(1)}, bf16[2,128,576]{1,2,0:T(8,128)(2,1)}, u32[]{:S(2)}) copy-start(bf16[2,128,576]{1,2,0:T(8,128)(2,1)} %param.10) | copy-start | bytes 884740
  3.3 0.7 %copy-start.2 = (bf16[2,3584]{1,0:T(2,128)(2,1)S(1)}, bf16[2,3584]{1,0:T(2,128)(2,1)}, u32[]{:S(2)}) copy-start(bf16[2,3584]{1,0:T(2,128)(2,1)} %tok_hbm.1) | copy-start | bytes 43012
  4.0 0.7 %copy-start.3 = (s32[2,8]{1,0:T(2,128)S(1)}, s32[2,8]{1,0:T(2,128)}, u32[]{:S(2)}) copy-start(s32[2,8]{1,0:T(2,128)} %rout_hbm.1) | copy-start | bytes 196
  4.7 0.7 %copy-start.4 = (f32[2,8]{1,0:T(2,128)S(1)}, f32[2,8]{1,0:T(2,128)}, u32[]{:S(2)}) copy-start(f32[2,8]{1,0:T(2,128)} %gw_hbm.1) | copy-start | bytes 196
  5.3 0.7 %copy-start.5 = (s32[64]{0:T(128)S(1)}, s32[64]{0:T(128)}, u32[]{:S(2)}) copy-start(s32[64]{0:T(128)} %lengths.1) | copy-start | bytes 772
  6.0 0.7 %copy-start.6 = (s32[16]{0:T(128)S(1)}, s32[16]{0:T(128)}, u32[]{:S(2)}) copy-start(s32[16]{0:T(128)} %trade_slot.1) | copy-start | bytes 196

commit v2 on v1

--- a/solution.py
+++ b/solution.py
@@ -43,9 +43,9 @@
 
 
 def kernel(
-    q_hbm, k_hbm, lengths, trade_slot, tok_hbm, rout_hbm, gw_hbm, wg_hbm, wu_hbm, wd_hbm,
+    q_hbm, k_hbm, len_hbm, trade_hbm, tok_hbm, rout_hbm, gw_hbm, wg_hbm, wu_hbm, wd_hbm,
     att_hbm, exp_ref,
-    tok, rout, gw, q, k, wg, wu, wd, stage, perm, gathered, q_out, q_in, o_out, o_in, att,
+    lengths, trade_slot, tok, rout, gw, q, k, wg, wu, wd, stage, perm, gathered, tok_rows, q_out, q_in, o_out, o_in, att,
     sums, mate_in, back, landed,
     small_sem, q_sem, k_sem, wg_sem, wu_sem, wd_sem, att_sem,
     tok_s, tok_r, fwd_s, fwd_r, trade_s, trade_r, mate_s, mate_r, back_s, back_r,
@@ -67,10 +67,12 @@
         pltpu.make_async_copy(tok_hbm, tok, small_sem.at[0]),
         pltpu.make_async_copy(rout_hbm, rout, small_sem.at[1]),
         pltpu.make_async_copy(gw_hbm, gw, small_sem.at[2]),
+        pltpu.make_async_copy(trade_hbm, trade_slot, small_sem.at[3]),
+        pltpu.make_async_copy(len_hbm, lengths, small_sem.at[4]),
         pltpu.make_async_copy(q_hbm, q, q_sem),
         pltpu.make_async_copy(k_hbm, k, k_sem),
     ]
-    tok_load, rout_load, gw_load, q_load, k_load = loads
+    tok_load, rout_load, gw_load, trade_load, len_load, q_load, k_load = loads
     wg_loads, wu_loads, wd_loads = [], [], []
     for s in range(PIECES):
         rows = pl.ds(s * W, W)
@@ -116,6 +118,8 @@
         copy.start()
     own_copy.start()
 
+    trade_load.wait()
+    len_load.wait()
     trade_at = trade_slot[me % 16]
     keep_at = 1 - trade_at
     q_load.wait()
@@ -137,28 +141,28 @@
         fwd_copies.append(send(block, block, fwd_s.at[i], fwd_r.at[i], mate))
         fwd_copies[i].start()
 
+    for copy in fwd_copies + [own_copy]:
+        copy.wait_recv()
+    rows = jnp.dot(perm[...], gathered[...].reshape(512, W), preferred_element_type=f32)
+    for s in range(PIECES):
+        tok_rows[s] = rows[s * 64 : (s + 1) * 64].astype(bf16)
+    lane = lax.broadcasted_iota(jnp.int32, (64, W), 1)
+    mine = (lane == me) | (lane == me + 32)
+    weight = jnp.sum(jnp.where(mine, rows[PIECES * 64 :], 0.0), axis=1, keepdims=True)
+
+    gate = jnp.zeros((64, 1024), f32)
+    up = jnp.zeros((64, 1024), f32)
+    for s in range(PIECES):
+        wg_loads[s].wait()
+        gate += jnp.dot(tok_rows[s], wg[s * W : (s + 1) * W, :], preferred_element_type=f32)
+        wu_loads[s].wait()
+        up += jnp.dot(tok_rows[s], wu[s * W : (s + 1) * W, :], preferred_element_type=f32)
+    hidden = (gate / (1.0 + jnp.exp(-gate)) * up).astype(bf16)
+
     q_copy.wait_recv()
     o_out[...] = attend(q_in[...], k[trade_at], lengths[me * 2 + trade_at])
     o_copy = send(o_out, o_in, trade_s.at[1], trade_r.at[1], partner)
     o_copy.start()
-
-    for copy in fwd_copies + [own_copy]:
-        copy.wait_recv()
-    rows = gathered[...].reshape(512, W)
-
-    gate = jnp.zeros((64, 1024), f32)
-    up = jnp.zeros((64, 1024), f32)
-    for s in range(PIECES):
-        x = jnp.dot(perm[s * 64 : (s + 1) * 64, :], rows, preferred_element_type=f32).astype(bf16)
-        wg_loads[s].wait()
-        gate += jnp.dot(x, wg[s * W : (s + 1) * W, :], preferred_element_type=f32)
-        wu_loads[s].wait()
-        up += jnp.dot(x, wu[s * W : (s + 1) * W, :], preferred_element_type=f32)
-    factors = jnp.dot(perm[PIECES * 64 :, :], rows, preferred_element_type=f32)
-    lane = lax.broadcasted_iota(jnp.int32, (64, W), 1)
-    mine = (lane == me) | (lane == me + 32)
-    weight = jnp.sum(jnp.where(mine, factors, 0.0), axis=1, keepdims=True)
-    hidden = (gate / (1.0 + jnp.exp(-gate)) * up).astype(bf16)
 
     mate_copies = []
     for s in range(PIECES):
@@ -191,7 +195,6 @@
     for copy in back_copies:
         copy.start()
     landed[chip] = back[chip]
-
     o_copy.wait_recv()
     arrived = o_in[...]
     att[0] = jnp.where(trade_at == 0, arrived, kept)
@@ -214,8 +217,7 @@
 def local(
     queries, latent_cache, lengths, trade_slot, tokens, routing, gate_weights, w_gate, w_up, w_down
 ):
-    any_spec = pl.BlockSpec(memory_space=pl.ANY)
-    smem_spec = pl.BlockSpec(memory_space=pltpu.SMEM)
+    hbm_spec = pl.BlockSpec(memory_space=pltpu.HBM)
     dma = pltpu.SemaphoreType.DMA
     vmem = pltpu.VMEM
     attended, rows = pl.pallas_call(
@@ -224,9 +226,11 @@
             jax.ShapeDtypeStruct((2, 128, LAT), bf16),
             jax.ShapeDtypeStruct((16, W), bf16),
         ),
-        in_specs=[any_spec, any_spec, smem_spec, smem_spec] + [any_spec] * 6,
-        out_specs=(any_spec, pl.BlockSpec(memory_space=pltpu.VMEM)),
+        in_specs=[hbm_spec] * 10,
+        out_specs=(pl.BlockSpec(memory_space=pl.ANY), pl.BlockSpec(memory_space=pltpu.VMEM)),
         scratch_shapes=[
+            pltpu.SMEM((64,), jnp.int32),
+            pltpu.SMEM((16,), jnp.int32),
             vmem((2, 3584), bf16),
             vmem((2, 8), jnp.int32),
             vmem((2, 8), f32),
@@ -238,6 +242,7 @@
             vmem((16, W), f32),
             vmem((512, 512), bf16),
             vmem((2, 16, 16, W), bf16),
+            vmem((PIECES, 64, W), bf16),
             vmem((576, 128), bf16),
             vmem((576, 128), bf16),
             vmem((128, LAT), bf16),
@@ -247,7 +252,7 @@
             vmem((PIECES, 32, W), bf16),
             vmem((16, 16, W), bf16),
             vmem((16, 16, W), bf16),
-            dma((3,)),
+            dma((5,)),
             dma,
             dma,
             dma((PIECES,)),
@@ -266,7 +271,7 @@
             dma((15,)),
         ],
         compiler_params=pltpu.CompilerParams(
-            collective_id=0, has_side_effects=True, vmem_limit_bytes=50 * 2**20
+            collective_id=0, has_side_effects=True, vmem_limit_bytes=56 * 2**20
         ),
         cost_estimate=pl.CostEstimate(
             flops=2_000_000_000, bytes_accessed=25_000_000, transcendentals=400_000

time: 39.7 us -> 35.1 us (0.88)
  local copies, waits for them, and re-layouts: 7.31 us -> 3 us
    unnamed x17 -> x3, local copies, waits for them, and re-layouts: 7.31 us -> 3 us
where the time goes in v2:
time: 35.1 us; the launch traced here: 34.9 us
  Pallas kernels  31.3 us (89%)
  local copies, waits for them, and re-layouts  3 us (9%)
  between operations  0.64 us (2%)
    pallas_call x1, Pallas kernels, local(): pl.pallas_call(kernel, out_shape=(jax.ShapeDtypeStruct((2, 128, LAT), bf1...  31.3 us
    unnamed x3, local copies, waits for them, and re-layouts  3 us

profile of v2, /device:TPU:1, one launch (start us, length us, event | category | flops | bytes accessed | tf_op | source)
XLA Modules:
  0.0 34.9 jit_solution(2822392083506367848)
XLA Ops:
  0.6 31.3 %shard_map.113 = (bf16[2,128,512]{2,1,0:T(8,128)(2,1)}, bf16[16,512]{1,0:T(8,128)(2,1)}) custom-call(bf16[2,576,128]{2,1,0:T(8,128)(2,1)} %bitcast.7, bf16[2,576,1024]{2,1,0:T(8,128)(2,1)} %bitcast.6, s32[64]{0:T(128)} %len_hbm.1, s32[16]{0:T(128)} %trade_hbm.1, bf16[2,3584]{1,0:T(2,128)(2,1)} %tok_hbm.1, s32[2,8]{1,0:T(2,128)} %rout_hbm.1, f32[2,8]{1,0:T(2,128)} %gw_hbm.1, ...), custom_call_target="tpu_custom_call" | custom-call | flops 2000000000 | bytes 25000000 | tf_op jit(solution)/shard_map/pallas_call | solution.py:223
  31.9 0.7 %slice_bitcast_fusion = bf16[1,2,7,512]{3,2,1,0:T(8,128)(2,1)S(1)} fusion(bf16[2,8,512]{2,1,0:T(8,128)(2,1)} %bitcast.8), kind=kLoop, calls=%fused_computation | loop fusion | bytes 28672
  32.6 0.6 %copy.12 = bf16[1,2,7,512]{3,1,2,0:T(2,128)(2,1)} copy(bf16[1,2,7,512]{3,2,1,0:T(8,128)(2,1)S(1)} %slice_bitcast_fusion) | data formatting | bytes 28672
  33.2 1.7 %copy.14 = bf16[2,128,512]{2,1,0:T(8,128)(2,1)} copy(bf16[2,128,512]{2,1,0:T(8,128)(2,1)} %get-tuple-element.8) | data formatting | bytes 524288

commit v3 on v2

--- a/solution.py
+++ b/solution.py
@@ -44,10 +44,10 @@
 
 def kernel(
     q_hbm, k_hbm, len_hbm, trade_hbm, tok_hbm, rout_hbm, gw_hbm, wg_hbm, wu_hbm, wd_hbm,
-    att_hbm, exp_ref,
-    lengths, trade_slot, tok, rout, gw, q, k, wg, wu, wd, stage, perm, gathered, tok_rows, q_out, q_in, o_out, o_in, att,
+    att, exp_ref,
+    lengths, trade_slot, tok, rout, gw, q, k, wg, wu, wd, stage, perm, gathered, tok_rows, q_out, q_in, o_out, o_in,
     sums, mate_in, back, landed,
-    small_sem, q_sem, k_sem, wg_sem, wu_sem, wd_sem, att_sem,
+    small_sem, q_sem, k_sem, wg_sem, wu_sem, wd_sem,
     tok_s, tok_r, fwd_s, fwd_r, trade_s, trade_r, mate_s, mate_r, back_s, back_r,
 ):
     me = lax.axis_index("dev")
@@ -60,9 +60,6 @@
     from_chip = [((cx + 4 - dx) % 4) * 4 + (cz + 4 - dz) % 4 for dx, dz in away]
 
     barrier = pltpu.get_barrier_semaphore()
-    for other in [c * 2 + core for c in to_chip] + [mate]:
-        pl.semaphore_signal(barrier, inc=1, device_id={"dev": other}, device_id_type=MESH)
-
     loads = [
         pltpu.make_async_copy(tok_hbm, tok, small_sem.at[0]),
         pltpu.make_async_copy(rout_hbm, rout, small_sem.at[1]),
@@ -81,13 +78,12 @@
         wd_loads.append(
             pltpu.make_async_copy(wd_hbm.at[0, :, rows], wd.at[:, rows], wd_sem.at[s])
         )
-    for load in loads:
+    for load in loads[:3]:
         load.start()
-    for s in range(PIECES):
-        wg_loads[s].start()
-        wu_loads[s].start()
-    for s in range(PIECES):
-        wd_loads[s].start()
+    for other in [c * 2 + core for c in to_chip] + [mate]:
+        pl.semaphore_signal(barrier, inc=1, device_id={"dev": other}, device_id_type=MESH)
+    for load in loads[3:]:
+        load.start()
 
     tok_load.wait()
     rout_load.wait()
@@ -106,6 +102,9 @@
             stage[t * SLOTS + s : t * SLOTS + s + 1, :] = tokens[t : t + 1, s * W : (s + 1) * W]
         stage[t * SLOTS + PIECES : (t + 1) * SLOTS, :] = factor[t : t + 1]
     gathered[core, chip] = stage[...].astype(bf16)
+    for s in range(PIECES):
+        wg_loads[s].start()
+        wu_loads[s].start()
 
     pl.semaphore_wait(barrier, 16)
 
@@ -113,10 +112,8 @@
     tok_copies = [
         send(own, own, tok_s.at[i], tok_r.at[i], to_chip[i] * 2 + core) for i in range(15)
     ]
-    own_copy = send(own, own, fwd_s.at[15], fwd_r.at[15], mate)
     for copy in tok_copies:
         copy.start()
-    own_copy.start()
 
     trade_load.wait()
     len_load.wait()
@@ -134,14 +131,15 @@
     k_load.wait()
     kept = attend(q[keep_at], k[keep_at], lengths[me * 2 + keep_at])
 
-    fwd_copies = []
-    for i in range(15):
-        tok_copies[i].wait_recv()
-        block = gathered.at[core, from_chip[i]]
-        fwd_copies.append(send(block, block, fwd_s.at[i], fwd_r.at[i], mate))
-        fwd_copies[i].start()
-
-    for copy in fwd_copies + [own_copy]:
+    for s in range(PIECES):
+        wd_loads[s].start()
+    for copy in tok_copies:
+        copy.wait_recv()
+    mine = gathered.at[core]
+    fwd_copies = [send(mine, mine, fwd_s.at[0], fwd_r.at[0], mate)]
+    fwd_copies[0].start()
+
+    for copy in fwd_copies:
         copy.wait_recv()
     rows = jnp.dot(perm[...], gathered[...].reshape(512, W), preferred_element_type=f32)
     for s in range(PIECES):
@@ -199,8 +197,6 @@
     arrived = o_in[...]
     att[0] = jnp.where(trade_at == 0, arrived, kept)
     att[1] = jnp.where(trade_at == 1, arrived, kept)
-    att_copy = pltpu.make_async_copy(att, att_hbm, att_sem)
-    att_copy.start()
 
     for copy in back_copies:
         copy.wait_recv()
@@ -209,8 +205,7 @@
         total += landed[c].astype(f32)
     exp_ref[...] = total.astype(bf16)
 
-    att_copy.wait()
-    for copy in tok_copies + fwd_copies + mate_copies + back_copies + [own_copy, q_copy, o_copy]:
+    for copy in tok_copies + fwd_copies + mate_copies + back_copies + [q_copy, o_copy]:
         copy.wait_send()
 
 
@@ -223,11 +218,11 @@
     attended, rows = pl.pallas_call(
         kernel,
         out_shape=(
-            jax.ShapeDtypeStruct((2, 128, LAT), bf16),
-            jax.ShapeDtypeStruct((16, W), bf16),
+            pltpu.VMEM((2, 128, LAT), bf16),
+            pltpu.VMEM((16, W), bf16),
         ),
         in_specs=[hbm_spec] * 10,
-        out_specs=(pl.BlockSpec(memory_space=pl.ANY), pl.BlockSpec(memory_space=pltpu.VMEM)),
+        out_specs=(pl.BlockSpec(memory_space=pltpu.VMEM),) * 2,
         scratch_shapes=[
             pltpu.SMEM((64,), jnp.int32),
             pltpu.SMEM((16,), jnp.int32),
@@ -247,7 +242,6 @@
             vmem((576, 128), bf16),
             vmem((128, LAT), bf16),
             vmem((128, LAT), bf16),
-            vmem((2, 128, LAT), bf16),
             vmem((PIECES, 2, 32, W), bf16),
             vmem((PIECES, 32, W), bf16),
             vmem((16, 16, W), bf16),
@@ -258,7 +252,6 @@
             dma((PIECES,)),
             dma((PIECES,)),
             dma((PIECES,)),
-            dma,
             dma((15,)),
             dma((15,)),
             dma((16,)),
@@ -277,16 +270,21 @@
             flops=2_000_000_000, bytes_accessed=25_000_000, transcendentals=400_000
         ),
     )(
-        jnp.swapaxes(queries, 1, 2),
-        jnp.swapaxes(latent_cache, 1, 2),
-        lengths,
-        trade_slot,
-        tokens,
-        routing,
-        gate_weights,
-        w_gate,
-        w_up,
-        w_down,
+        *[
+            pltpu.with_memory_space_constraint(operand, pltpu.HBM)
+            for operand in (
+                jnp.swapaxes(queries, 1, 2),
+                jnp.swapaxes(latent_cache, 1, 2),
+                lengths,
+                trade_slot,
+                tokens,
+                routing,
+                gate_weights,
+                w_gate,
+                w_up,
+                w_down,
+            )
+        ]
     )
     expert_out = rows.reshape(2, SLOTS, W)[:, :PIECES].reshape(2, PIECES * W)
     return attended, expert_out

time: 35.1 us -> 30.7 us (0.87)
  Pallas kernels: 31.3 us -> 28.3 us
  local copies, waits for them, and re-layouts: 3 us -> 1.32 us
    pallas_call x1, Pallas kernels: 31.3 us -> 28.3 us  [local(): pl.pallas_call(kernel, out_shape=(pltpu.VMEM((2, 128, LAT), bf16), pltpu....]
    unnamed x3, local copies, waits for them, and re-layouts: 3 us -> 1.32 us
where the time goes in v3:
time: 30.7 us; the launch traced here: 30.2 us
  Pallas kernels  28.3 us (92%)
  local copies, waits for them, and re-layouts  1.32 us (4%)
  between operations  0.64 us (2%)
    pallas_call x1, Pallas kernels, local(): pl.pallas_call(kernel, out_shape=(pltpu.VMEM((2, 128, LAT), bf16), pltpu....  28.3 us
    unnamed x3, local copies, waits for them, and re-layouts  1.32 us

profile of v3, /device:TPU:1, one launch (start us, length us, event | category | flops | bytes accessed | tf_op | source)
XLA Modules:
  0.0 30.2 jit_solution(17194289844665818994)
XLA Ops:
  0.6 28.3 %shard_map.113 = (bf16[2,128,512]{2,1,0:T(8,128)(2,1)S(1)}, bf16[16,512]{1,0:T(8,128)(2,1)S(1)}) custom-call(bf16[2,576,128]{2,1,0:T(8,128)(2,1)} %bitcast.8, bf16[2,576,1024]{2,1,0:T(8,128)(2,1)} %bitcast.7, s32[64]{0:T(128)} %len_hbm.1, s32[16]{0:T(128)} %trade_hbm.1, bf16[2,3584]{1,0:T(2,128)(2,1)} %tok_hbm.1, s32[2,8]{1,0:T(2,128)} %rout_hbm.1, ...), custom_call_target="tpu_custom_call" | custom-call | flops 2000000000 | bytes 25000000 | tf_op jit(solution)/shard_map/pallas_call | solution.py:218
  28.9 0.7 %copy.14 = bf16[2,128,512]{2,1,0:T(8,128)(2,1)} copy(bf16[2,128,512]{2,1,0:T(8,128)(2,1)S(1)} %get-tuple-element.6) | data formatting | bytes 524288
  29.6 0.6 %copy.12 = bf16[1,2,7,512]{3,1,2,0:T(2,128)(2,1)} copy(bf16[1,2,7,512]{3,2,1,0:T(8,128)(2,1)S(1)} %slice_bitcast_fusion) | data formatting | bytes 28672
  (1 shorter events, 0.0 us)

commit v4 on v3

v4 whole, which is shorter than its diff:
```python
import functools

import jax
import jax.numpy as jnp
from jax import lax
from jax.experimental import pallas as pl
from jax.experimental.pallas import tpu as pltpu
from jax.sharding import PartitionSpec as P

LAT = 512
W = 512
CUTS = ((0, 4), (4, 7))
BATCHES = ((0, 16),)
PIECES = 7
SLOTS = 8
score_scale = 192.0 ** (-0.5)
MESH = pl.DeviceIdType.MESH
f32 = jnp.float32
bf16 = jnp.bfloat16


def send(src, dst, send_sem, recv_sem, to):
    return pltpu.make_async_remote_copy(
        src_ref=src,
        dst_ref=dst,
        send_sem=send_sem,
        recv_sem=recv_sem,
        device_id={"dev": to},
        device_id_type=MESH,
    )


def attend(q_t, k_t, live):
    scores = (
        lax.dot_general(q_t, k_t, (((0,), (0,)), ((), ())), preferred_element_type=f32)
        * score_scale
    )
    position = lax.broadcasted_iota(jnp.int32, scores.shape, 1)
    scores = jnp.where(position < live, scores, -jnp.inf)
    weights = jnp.exp(scores - jnp.max(scores, axis=1, keepdims=True))
    shares = (weights / jnp.sum(weights, axis=1, keepdims=True)).astype(bf16)
    return lax.dot_general(
        shares, k_t[:LAT], (((1,), (1,)), ((), ())), preferred_element_type=f32
    ).astype(bf16)


def kernel(
    q_hbm, k_hbm, len_hbm, trade_hbm, tok_hbm, rout_hbm, gw_hbm, wg_hbm, wu_hbm, wd_hbm,
    att, exp_ref,
    lengths, trade_slot, tok, rout, gw, q, k, wg, wu, wd, stage, perm, gathered, tok_rows, factors,
    q_out, q_in, o_out, o_in, sums, mate_in, back, landed,
    small_sem, q_sem, k_sem, wg_sem, wu_sem, wd_sem,
    tok_s, tok_r, fwd_s, fwd_r, trade_s, trade_r, mate_s, mate_r, back_s, back_r,
):
    me = lax.axis_index("dev")
    chip, core = lax.div(me, 2), lax.rem(me, 2)
    cx, cz = lax.div(chip, 4), lax.rem(chip, 4)
    other_core = 1 - core
    mate = chip * 2 + other_core
    partner = lax.rem(me + 16, 32)
    xs = [cx] + [lax.rem(cx + d, 4) for d in (1, 2, 3)]
    zs = [cz] + [lax.rem(cz + d, 4) for d in (1, 2, 3)]
    away = [(dx, dz) for dx in (2, 1, 3, 0) for dz in (2, 1, 3, 0) if (dx, dz) != (0, 0)]
    to = [(xs[dx] * 4 + zs[dz]) * 2 + core for dx, dz in away]
    source = [(xs[(4 - dx) % 4] * 4 + zs[(4 - dz) % 4]) * 2 + core for dx, dz in away]

    loads = [
        pltpu.make_async_copy(tok_hbm, tok, small_sem.at[0]),
        pltpu.make_async_copy(rout_hbm, rout, small_sem.at[1]),
        pltpu.make_async_copy(gw_hbm, gw, small_sem.at[2]),
        pltpu.make_async_copy(trade_hbm, trade_slot, small_sem.at[3]),
        pltpu.make_async_copy(len_hbm, lengths, small_sem.at[4]),
        pltpu.make_async_copy(q_hbm, q, q_sem),
        pltpu.make_async_copy(k_hbm, k, k_sem),
    ]
    tok_load, rout_load, gw_load, trade_load, len_load, q_load, k_load = loads
    wg_loads, wu_loads, wd_loads = [], [], []
    for i, (first, last) in enumerate(CUTS):
        rows = pl.ds(first * W, (last - first) * W)
        wg_loads.append(pltpu.make_async_copy(wg_hbm.at[0, rows], wg.at[rows], wg_sem.at[i]))
        wu_loads.append(pltpu.make_async_copy(wu_hbm.at[0, rows], wu.at[rows], wu_sem.at[i]))
        wd_loads.append(
            pltpu.make_async_copy(wd_hbm.at[0, :, rows], wd.at[:, rows], wd_sem.at[i])
        )
    for load in loads[:3]:
        load.start()
    barrier = pltpu.get_barrier_semaphore()
    for other in to + [mate]:
        pl.semaphore_signal(barrier, inc=1, device_id={"dev": other}, device_id_type=MESH)
    for load in loads[3:]:
        load.start()

    row = lax.broadcasted_iota(jnp.int32, (256, 256), 0)
    col = lax.broadcasted_iota(jnp.int32, (256, 256), 1)
    perm[0] = jnp.where(col == (row % 32) * SLOTS + row // 32, 1.0, 0.0).astype(bf16)
    perm[1] = jnp.where(row == (col % 32) * SLOTS + col // 32, 1.0, 0.0).astype(bf16)

    tok_load.wait()
    rout_load.wait()
    gw_load.wait()
    tokens = tok[...].astype(f32)
    lane = lax.broadcasted_iota(jnp.int32, (2, W), 1)
    factor = jnp.zeros((2, W), f32)
    for top in range(8):
        expert, weight = rout[:, top : top + 1], gw[:, top : top + 1]
        hit = (lane == expert) | (lane == expert + 32)
        factor = factor + jnp.where(hit, weight, 0.0)
    high = factor.astype(bf16).astype(f32)
    factor = jnp.where(lane < 32, high, factor - high)
    for t in range(2):
        for s in range(PIECES):
            stage[t * SLOTS + s : t * SLOTS + s + 1, :] = tokens[t : t + 1, s * W : (s + 1) * W]
        stage[t * SLOTS + PIECES : (t + 1) * SLOTS, :] = factor[t : t + 1]
    gathered[core, 15] = stage[...].astype(bf16)
    for i in range(2):
        wg_loads[i].start()
        wu_loads[i].start()

    pl.semaphore_wait(barrier, 16)

    own = gathered.at[core, 15]
    tok_copies = [
        send(own, gathered.at[core, i], tok_s.at[i], tok_r.at[i], to[i]) for i in range(15)
    ]
    for copy in tok_copies:
        copy.start()

    trade_load.wait()
    len_load.wait()
    trade_at = trade_slot[me % 16]
    keep_at = 1 - trade_at
    q_load.wait()
    q_out[...] = q[trade_at]
    q_copy = send(q_out, q_in, trade_s.at[0], trade_r.at[0], partner)

    k_load.wait()
    kept = attend(q[keep_at], k[keep_at], lengths[me * 2 + keep_at])
    q_copy.start()
    for i in range(2):
        wd_loads[i].start()

    def spread(side):
        rows = jnp.dot(
            perm[0], gathered[side].reshape(256, W), preferred_element_type=f32
        )
        for s in range(PIECES):
            tok_rows[s, side] = rows[s * 32 : (s + 1) * 32].astype(bf16)
        factors[side] = rows[PIECES * 32 :]

    fwd_copies = []
    for i, (first, last) in enumerate(BATCHES):
        for copy in tok_copies[first : min(last, 15)]:
            copy.wait_recv()
        batch = gathered.at[core, pl.ds(first, last - first)]
        fwd_copies.append(send(batch, batch, fwd_s.at[i], fwd_r.at[i], mate))
        fwd_copies[i].start()
    spread(core)
    for copy in fwd_copies:
        copy.wait_recv()
    spread(other_core)

    gate = jnp.zeros((64, 1024), f32)
    up = jnp.zeros((64, 1024), f32)
    for i, (first, last) in enumerate(CUTS):
        wg_loads[i].wait()
        wu_loads[i].wait()
        for s in range(first, last):
            x = tok_rows[s].reshape(64, W)
            rows = slice(s * W, (s + 1) * W)
            gate += jnp.dot(x, wg[rows, :], preferred_element_type=f32)
            up += jnp.dot(x, wu[rows, :], preferred_element_type=f32)
    hidden = (gate / (1.0 + jnp.exp(-gate)) * up).astype(bf16)
    lane = lax.broadcasted_iota(jnp.int32, (64, W), 1)
    mine = (lane == me) | (lane == me + 32)
    weight = jnp.sum(jnp.where(mine, factors[...].reshape(64, W), 0.0), axis=1, keepdims=True)

    q_copy.wait_recv()
    o_out[...] = attend(q_in[...], k[trade_at], lengths[me * 2 + trade_at])
    o_copy = send(o_out, o_in, trade_s.at[1], trade_r.at[1], partner)
    o_copy.start()

    mate_copies = []
    for i, (first, last) in enumerate(CUTS):
        wd_loads[i].wait()
        for s in range(first, last):
            y = jnp.dot(hidden, wd[:, s * W : (s + 1) * W], preferred_element_type=f32)
            y = (y.astype(bf16).astype(f32) * weight).astype(bf16)
            sums[0, s] = y[:32]
            sums[1, s] = y[32:]
        cut = pl.ds(first, last - first)
        mate_copies.append(
            send(sums.at[other_core, cut], mate_in.at[cut], mate_s.at[i], mate_r.at[i], mate)
        )
        mate_copies[i].start()
    for copy in mate_copies:
        copy.wait_recv()
    part = (sums[core].astype(f32) + mate_in[...].astype(f32)).astype(bf16)
    part = jnp.concatenate([part.reshape(PIECES * 32, W), jnp.zeros((32, W), bf16)], axis=0)
    back[...] = (
        jnp.dot(perm[1], part, preferred_element_type=f32).astype(bf16).reshape(16, 16, W)
    )
    back_copies = [
        send(back.at[i], landed.at[i], back_s.at[i], back_r.at[i], source[i])
        for i in range(15)
    ]
    for copy in back_copies:
        copy.start()

    for copy in tok_copies + mate_copies + fwd_copies + [q_copy, o_copy]:
        copy.wait_send()
    o_copy.wait_recv()
    arrived = o_in[...]
    att[0] = jnp.where(trade_at == 0, arrived, kept)
    att[1] = jnp.where(trade_at == 1, arrived, kept)

    for copy in back_copies:
        copy.wait_recv()
    total = back[15].astype(f32)
    for i in range(15):
        total += landed[i].astype(f32)
    exp_ref[...] = total.astype(bf16)
    for copy in back_copies:
        copy.wait_send()


def finish(att_ref, row_ref, att_hbm, exp_hbm, line, exp, sem):
    att_copy = pltpu.make_async_copy(att_ref, att_hbm, sem.at[0])
    att_copy.start()
    rows = row_ref[...].astype(f32)
    for t in range(2):
        for s in range(PIECES):
            line[t : t + 1, s * W : (s + 1) * W] = rows[t * SLOTS + s : t * SLOTS + s + 1]
    exp[...] = line[...].astype(bf16)
    exp_copy = pltpu.make_async_copy(exp, exp_hbm, sem.at[1])
    exp_copy.start()
    att_copy.wait()
    exp_copy.wait()


def local(
    queries, latent_cache, lengths, trade_slot, tokens, routing, gate_weights, w_gate, w_up, w_down
):
    hbm_spec = pl.BlockSpec(memory_space=pltpu.HBM)
    dma = pltpu.SemaphoreType.DMA
    vmem = pltpu.VMEM
    attended, rows = pl.pallas_call(
        kernel,
        out_shape=(
            pltpu.VMEM((2, 128, LAT), bf16),
            pltpu.VMEM((16, W), bf16),
        ),
        in_specs=[hbm_spec] * 10,
        out_specs=(pl.BlockSpec(memory_space=pltpu.VMEM),) * 2,
        scratch_shapes=[
            pltpu.SMEM((64,), jnp.int32),
            pltpu.SMEM((16,), jnp.int32),
            vmem((2, 3584), bf16),
            vmem((2, 8), jnp.int32),
            vmem((2, 8), f32),
            vmem((2, 576, 128), bf16),
            vmem((2, 576, 1024), bf16),
            vmem((3584, 1024), bf16),
            vmem((3584, 1024), bf16),
            vmem((1024, 3584), bf16),
            vmem((16, W), f32),
            vmem((2, 256, 256), bf16),
            vmem((2, 16, 16, W), bf16),
            vmem((PIECES, 2, 32, W), bf16),
            vmem((2, 32, W), f32),
            vmem((576, 128), bf16),
            vmem((576, 128), bf16),
            vmem((128, LAT), bf16),
            vmem((128, LAT), bf16),
            vmem((2, PIECES, 32, W), bf16),
            vmem((PIECES, 32, W), bf16),
            vmem((16, 16, W), bf16),
            vmem((15, 16, W), bf16),
            dma((5,)),
            dma,
            dma,
            dma((2,)),
            dma((2,)),
            dma((2,)),
            dma((15,)),
            dma((15,)),
            dma((2,)),
            dma((2,)),
            dma((2,)),
            dma((2,)),
            dma((2,)),
            dma((2,)),
            dma((15,)),
            dma((15,)),
        ],
        compiler_params=pltpu.CompilerParams(
            collective_id=0, has_side_effects=True, vmem_limit_bytes=56 * 2**20
        ),
        cost_estimate=pl.CostEstimate(
            flops=2_000_000_000, bytes_accessed=25_000_000, transcendentals=400_000
        ),
    )(
        *[
            pltpu.with_memory_space_constraint(operand, pltpu.HBM)
            for operand in (
                jnp.swapaxes(queries, 1, 2),
                jnp.swapaxes(latent_cache, 1, 2),
                lengths,
                trade_slot,
                tokens,
                routing,
                gate_weights,
                w_gate,
                w_up,
                w_down,
            )
        ]
    )
    return pl.pallas_call(
        finish,
        out_shape=(pltpu.HBM((2, 128, LAT), bf16), pltpu.HBM((2, PIECES * W), bf16)),
        in_specs=[pl.BlockSpec(memory_space=pltpu.VMEM)] * 2,
        out_specs=(hbm_spec,) * 2,
        scratch_shapes=[vmem((2, PIECES * W), f32), vmem((2, PIECES * W), bf16), dma((2,))],
    )(
        pltpu.with_memory_space_constraint(attended, pltpu.VMEM),
        pltpu.with_memory_space_constraint(rows, pltpu.VMEM),
    )


def solution(mesh):
    in_specs = (
        P(("rep", "dev"), None, None),
        P(("rep", "dev"), None, None),
        P("rep"),
        P("rep"),
        P(("rep", "dev"), None),
        P(("rep", "dev"), None),
        P(("rep", "dev"), None),
        P("dev", None, None),
        P("dev", None, None),
        P("dev", None, None),
    )
    out_specs = (P(("rep", "dev"), None, None), P(("rep", "dev"), None))
    return jax.shard_map(local, mesh=mesh, in_specs=in_specs, out_specs=out_specs, check_vma=False)
```

time: 30.7 us -> 28.9 us (0.941)
  local copies, waits for them, and re-layouts: 1.32 us -> 0 us
  Pallas kernels: 28.3 us -> 27.8 us
    unnamed x3 -> x0, local copies, waits for them, and re-layouts: 1.32 us -> none
    pallas_call x1, Pallas kernels: 28.3 us -> 27.1 us  [local(): pl.pallas_call(kernel, out_shape=(pltpu.VMEM((2, 128, LAT), bf16), pltpu....]
    pallas_call x0 -> x1, Pallas kernels: none -> 0.72 us  [local(): pl.pallas_call(finish, out_shape=(pltpu.HBM((2, 128, LAT), bf16), pltpu.H...]
where the time goes in v4:
time: 28.9 us; the launch traced here: 28.5 us
  Pallas kernels  27.8 us (96%)
  between operations  0.64 us (2%)
    pallas_call x1, Pallas kernels, local(): pl.pallas_call(kernel, out_shape=(pltpu.VMEM((2, 128, LAT), bf16), pltpu....  27.1 us
    pallas_call x1, Pallas kernels, local(): pl.pallas_call(finish, out_shape=(pltpu.HBM((2, 128, LAT), bf16), pltpu.H...  0.72 us

profile of v4, /device:TPU:1, one launch (start us, length us, event | category | flops | bytes accessed | tf_op | source)
XLA Modules:
  0.0 28.5 jit_solution(8953482538892014203)
XLA Ops:
  0.6 27.1 %shard_map.113 = (bf16[2,128,512]{2,1,0:T(8,128)(2,1)S(1)}, bf16[16,512]{1,0:T(8,128)(2,1)S(1)}) custom-call(bf16[2,576,128]{2,1,0:T(8,128)(2,1)} %bitcast.3, bf16[2,576,1024]{2,1,0:T(8,128)(2,1)} %bitcast.2, s32[64]{0:T(128)} %len_hbm.1, s32[16]{0:T(128)} %trade_hbm.1, bf16[2,3584]{1,0:T(2,128)(2,1)} %tok_hbm.1, s32[2,8]{1,0:T(2,128)} %rout_hbm.1, ...), custom_call_target="tpu_custom_call" | custom-call | flops 2000000000 | bytes 25000000 | tf_op jit(solution)/shard_map/pallas_call | solution.py:246
  27.7 0.7 %shard_map.114 = (bf16[2,128,512]{2,1,0:T(8,128)(2,1)}, bf16[2,3584]{1,0:T(2,128)(2,1)}) custom-call(bf16[2,128,512]{2,1,0:T(8,128)(2,1)S(1)} %get-tuple-element.4.att_ref, bf16[16,512]{1,0:T(8,128)(2,1)S(1)} %get-tuple-element.5.row_ref), custom_call_target="tpu_custom_call" | custom-call | tf_op jit(solution)/shard_map/pallas_call | solution.py:318

commit v5 on v4

--- a/solution.py
+++ b/solution.py
@@ -28,6 +28,10 @@
         device_id={"dev": to},
         device_id_type=MESH,
     )
+
+
+def all_fifteen(blocks, sem):
+    pltpu.make_async_copy(blocks, blocks, sem).wait()
 
 
 def attend(q_t, k_t, live):
@@ -90,6 +94,7 @@
     for load in loads[3:]:
         load.start()
 
+    tok_rows[:, 2:] = jnp.zeros((PIECES, 2, 32, W), bf16)
     row = lax.broadcasted_iota(jnp.int32, (256, 256), 0)
     col = lax.broadcasted_iota(jnp.int32, (256, 256), 1)
     perm[0] = jnp.where(col == (row % 32) * SLOTS + row // 32, 1.0, 0.0).astype(bf16)
@@ -120,7 +125,7 @@
 
     own = gathered.at[core, 15]
     tok_copies = [
-        send(own, gathered.at[core, i], tok_s.at[i], tok_r.at[i], to[i]) for i in range(15)
+        send(own, gathered.at[core, i], tok_s, tok_r, to[i]) for i in range(15)
     ]
     for copy in tok_copies:
         copy.start()
@@ -149,8 +154,7 @@
 
     fwd_copies = []
     for i, (first, last) in enumerate(BATCHES):
-        for copy in tok_copies[first : min(last, 15)]:
-            copy.wait_recv()
+        all_fifteen(gathered.at[core, pl.ds(0, 15)], tok_r)
         batch = gathered.at[core, pl.ds(first, last - first)]
         fwd_copies.append(send(batch, batch, fwd_s.at[i], fwd_r.at[i], mate))
         fwd_copies[i].start()
@@ -159,17 +163,19 @@
         copy.wait_recv()
     spread(other_core)
 
-    gate = jnp.zeros((64, 1024), f32)
-    up = jnp.zeros((64, 1024), f32)
+    gate = jnp.zeros((128, 1024), f32)
+    up = jnp.zeros((128, 1024), f32)
     for i, (first, last) in enumerate(CUTS):
         wg_loads[i].wait()
         wu_loads[i].wait()
         for s in range(first, last):
-            x = tok_rows[s].reshape(64, W)
+            x = tok_rows[s].reshape(128, W)
             rows = slice(s * W, (s + 1) * W)
             gate += jnp.dot(x, wg[rows, :], preferred_element_type=f32)
             up += jnp.dot(x, wu[rows, :], preferred_element_type=f32)
+    gate, up = gate[:64], up[:64]
     hidden = (gate / (1.0 + jnp.exp(-gate)) * up).astype(bf16)
+    hidden = jnp.concatenate([hidden, jnp.zeros((64, 1024), bf16)], axis=0)
     lane = lax.broadcasted_iota(jnp.int32, (64, W), 1)
     mine = (lane == me) | (lane == me + 32)
     weight = jnp.sum(jnp.where(mine, factors[...].reshape(64, W), 0.0), axis=1, keepdims=True)
@@ -183,7 +189,7 @@
     for i, (first, last) in enumerate(CUTS):
         wd_loads[i].wait()
         for s in range(first, last):
-            y = jnp.dot(hidden, wd[:, s * W : (s + 1) * W], preferred_element_type=f32)
+            y = jnp.dot(hidden, wd[:, s * W : (s + 1) * W], preferred_element_type=f32)[:64]
             y = (y.astype(bf16).astype(f32) * weight).astype(bf16)
             sums[0, s] = y[:32]
             sums[1, s] = y[32:]
@@ -200,27 +206,26 @@
         jnp.dot(perm[1], part, preferred_element_type=f32).astype(bf16).reshape(16, 16, W)
     )
     back_copies = [
-        send(back.at[i], landed.at[i], back_s.at[i], back_r.at[i], source[i])
+        send(back.at[i], landed.at[i], back_s, back_r, source[i])
         for i in range(15)
     ]
     for copy in back_copies:
         copy.start()
 
-    for copy in tok_copies + mate_copies + fwd_copies + [q_copy, o_copy]:
+    all_fifteen(gathered.at[core, pl.ds(0, 15)], tok_s)
+    for copy in mate_copies + fwd_copies + [q_copy, o_copy]:
         copy.wait_send()
     o_copy.wait_recv()
     arrived = o_in[...]
     att[0] = jnp.where(trade_at == 0, arrived, kept)
     att[1] = jnp.where(trade_at == 1, arrived, kept)
 
-    for copy in back_copies:
-        copy.wait_recv()
+    all_fifteen(landed, back_r)
     total = back[15].astype(f32)
     for i in range(15):
         total += landed[i].astype(f32)
     exp_ref[...] = total.astype(bf16)
-    for copy in back_copies:
-        copy.wait_send()
+    all_fifteen(landed, back_s)
 
 
 def finish(att_ref, row_ref, att_hbm, exp_hbm, line, exp, sem):
@@ -265,7 +270,7 @@
             vmem((16, W), f32),
             vmem((2, 256, 256), bf16),
             vmem((2, 16, 16, W), bf16),
-            vmem((PIECES, 2, 32, W), bf16),
+            vmem((PIECES, 4, 32, W), bf16),
             vmem((2, 32, W), f32),
             vmem((576, 128), bf16),
             vmem((576, 128), bf16),
@@ -281,16 +286,16 @@
             dma((2,)),
             dma((2,)),
             dma((2,)),
-            dma((15,)),
-            dma((15,)),
-            dma((2,)),
-            dma((2,)),
-            dma((2,)),
-            dma((2,)),
-            dma((2,)),
-            dma((2,)),
-            dma((15,)),
-            dma((15,)),
+            dma,
+            dma,
+            dma((2,)),
+            dma((2,)),
+            dma((2,)),
+            dma((2,)),
+            dma((2,)),
+            dma((2,)),
+            dma,
+            dma,
         ],
         compiler_params=pltpu.CompilerParams(
             collective_id=0, has_side_effects=True, vmem_limit_bytes=56 * 2**20

time: 28.9 us -> 27.9 us (0.965)
  Pallas kernels: 27.8 us -> 27.1 us
    pallas_call x1, Pallas kernels: 27.1 us -> 26.4 us  [local(): pl.pallas_call(kernel, out_shape=(pltpu.VMEM((2, 128, LAT), bf16), pltpu....]
where the time goes in v5:
time: 27.9 us; the launch traced here: 27.7 us
  Pallas kernels  27.1 us (97%)
  between operations  0.64 us (2%)
    pallas_call x1, Pallas kernels, local(): pl.pallas_call(kernel, out_shape=(pltpu.VMEM((2, 128, LAT), bf16), pltpu....  26.4 us
    pallas_call x1, Pallas kernels, local(): pl.pallas_call(finish, out_shape=(pltpu.HBM((2, 128, LAT), bf16), pltpu.H...  0.72 us

profile of v5, /device:TPU:1, one launch (start us, length us, event | category | flops | bytes accessed | tf_op | source)
XLA Modules:
  0.0 27.7 jit_solution(12659814329319097968)
XLA Ops:
  0.6 26.4 %shard_map.113 = (bf16[2,128,512]{2,1,0:T(8,128)(2,1)S(1)}, bf16[16,512]{1,0:T(8,128)(2,1)S(1)}) custom-call(bf16[2,576,128]{2,1,0:T(8,128)(2,1)} %bitcast.3, bf16[2,576,1024]{2,1,0:T(8,128)(2,1)} %bitcast.2, s32[64]{0:T(128)} %len_hbm.1, s32[16]{0:T(128)} %trade_hbm.1, bf16[2,3584]{1,0:T(2,128)(2,1)} %tok_hbm.1, s32[2,8]{1,0:T(2,128)} %rout_hbm.1, ...), custom_call_target="tpu_custom_call" | custom-call | flops 2000000000 | bytes 25000000 | tf_op jit(solution)/shard_map/pallas_call | solution.py:251
  27.0 0.7 %shard_map.114 = (bf16[2,128,512]{2,1,0:T(8,128)(2,1)}, bf16[2,3584]{1,0:T(2,128)(2,1)}) custom-call(bf16[2,128,512]{2,1,0:T(8,128)(2,1)S(1)} %get-tuple-element.4.att_ref, bf16[16,512]{1,0:T(8,128)(2,1)S(1)} %get-tuple-element.5.row_ref), custom_call_target="tpu_custom_call" | custom-call | tf_op jit(solution)/shard_map/pallas_call | solution.py:323

commit v6 on v5

--- a/solution.py
+++ b/solution.py
@@ -64,7 +64,8 @@
     partner = lax.rem(me + 16, 32)
     xs = [cx] + [lax.rem(cx + d, 4) for d in (1, 2, 3)]
     zs = [cz] + [lax.rem(cz + d, 4) for d in (1, 2, 3)]
-    away = [(dx, dz) for dx in (2, 1, 3, 0) for dz in (2, 1, 3, 0) if (dx, dz) != (0, 0)]
+    away = [(2, 2), (2, 1), (1, 2), (2, 3), (3, 2), (2, 0), (0, 2), (1, 1), (3, 3), (1, 3), (3, 1)]
+    away += [(1, 0), (0, 1), (3, 0), (0, 3)]
     to = [(xs[dx] * 4 + zs[dz]) * 2 + core for dx, dz in away]
     source = [(xs[(4 - dx) % 4] * 4 + zs[(4 - dz) % 4]) * 2 + core for dx, dz in away]
 
@@ -94,12 +95,6 @@
     for load in loads[3:]:
         load.start()
 
-    tok_rows[:, 2:] = jnp.zeros((PIECES, 2, 32, W), bf16)
-    row = lax.broadcasted_iota(jnp.int32, (256, 256), 0)
-    col = lax.broadcasted_iota(jnp.int32, (256, 256), 1)
-    perm[0] = jnp.where(col == (row % 32) * SLOTS + row // 32, 1.0, 0.0).astype(bf16)
-    perm[1] = jnp.where(row == (col % 32) * SLOTS + col // 32, 1.0, 0.0).astype(bf16)
-
     tok_load.wait()
     rout_load.wait()
     gw_load.wait()
@@ -130,6 +125,12 @@
     for copy in tok_copies:
         copy.start()
 
+    tok_rows[:, 2:] = jnp.zeros((PIECES, 2, 32, W), bf16)
+    row = lax.broadcasted_iota(jnp.int32, (256, 256), 0)
+    col = lax.broadcasted_iota(jnp.int32, (256, 256), 1)
+    perm[0] = jnp.where(col == (row & 31) * SLOTS + (row >> 5), 1.0, 0.0).astype(bf16)
+    perm[1] = jnp.where(row == (col & 31) * SLOTS + (col >> 5), 1.0, 0.0).astype(bf16)
+
     trade_load.wait()
     len_load.wait()
     trade_at = trade_slot[me % 16]
@@ -137,10 +138,10 @@
     q_load.wait()
     q_out[...] = q[trade_at]
     q_copy = send(q_out, q_in, trade_s.at[0], trade_r.at[0], partner)
+    q_copy.start()
 
     k_load.wait()
     kept = attend(q[keep_at], k[keep_at], lengths[me * 2 + keep_at])
-    q_copy.start()
     for i in range(2):
         wd_loads[i].start()
 
@@ -166,6 +167,11 @@
     gate = jnp.zeros((128, 1024), f32)
     up = jnp.zeros((128, 1024), f32)
     for i, (first, last) in enumerate(CUTS):
+        if i == 1:
+            q_copy.wait_recv()
+            o_out[...] = attend(q_in[...], k[trade_at], lengths[me * 2 + trade_at])
+            o_copy = send(o_out, o_in, trade_s.at[1], trade_r.at[1], partner)
+            o_copy.start()
         wg_loads[i].wait()
         wu_loads[i].wait()
         for s in range(first, last):
@@ -179,11 +185,6 @@
     lane = lax.broadcasted_iota(jnp.int32, (64, W), 1)
     mine = (lane == me) | (lane == me + 32)
     weight = jnp.sum(jnp.where(mine, factors[...].reshape(64, W), 0.0), axis=1, keepdims=True)
-
-    q_copy.wait_recv()
-    o_out[...] = attend(q_in[...], k[trade_at], lengths[me * 2 + trade_at])
-    o_copy = send(o_out, o_in, trade_s.at[1], trade_r.at[1], partner)
-    o_copy.start()
 
     mate_copies = []
     for i, (first, last) in enumerate(CUTS):

time: 27.9 us -> 27.3 us (0.978)
  Pallas kernels: 27.1 us -> 26.5 us
    pallas_call x1, Pallas kernels: 26.4 us -> 25.8 us  [local(): pl.pallas_call(kernel, out_shape=(pltpu.VMEM((2, 128, LAT), bf16), pltpu....]
where the time goes in v6:
time: 27.3 us; the launch traced here: 27.2 us
  Pallas kernels  26.5 us (97%)
  between operations  0.64 us (2%)
    pallas_call x1, Pallas kernels, local(): pl.pallas_call(kernel, out_shape=(pltpu.VMEM((2, 128, LAT), bf16), pltpu....  25.8 us
    pallas_call x1, Pallas kernels, local(): pl.pallas_call(finish, out_shape=(pltpu.HBM((2, 128, LAT), bf16), pltpu.H...  0.72 us

profile of v6, /device:TPU:1, one launch (start us, length us, event | category | flops | bytes accessed | tf_op | source)
XLA Modules:
  0.0 27.2 jit_solution(7671134020844579349)
XLA Ops:
  0.6 25.8 %shard_map.113 = (bf16[2,128,512]{2,1,0:T(8,128)(2,1)S(1)}, bf16[16,512]{1,0:T(8,128)(2,1)S(1)}) custom-call(bf16[2,576,128]{2,1,0:T(8,128)(2,1)} %bitcast.3, bf16[2,576,1024]{2,1,0:T(8,128)(2,1)} %bitcast.2, s32[64]{0:T(128)} %len_hbm.1, s32[16]{0:T(128)} %trade_hbm.1, bf16[2,3584]{1,0:T(2,128)(2,1)} %tok_hbm.1, s32[2,8]{1,0:T(2,128)} %rout_hbm.1, ...), custom_call_target="tpu_custom_call" | custom-call | flops 2000000000 | bytes 25000000 | tf_op jit(solution)/shard_map/pallas_call | solution.py:252
  26.4 0.7 %shard_map.114 = (bf16[2,128,512]{2,1,0:T(8,128)(2,1)}, bf16[2,3584]{1,0:T(2,128)(2,1)}) custom-call(bf16[2,128,512]{2,1,0:T(8,128)(2,1)S(1)} %get-tuple-element.4.att_ref, bf16[16,512]{1,0:T(8,128)(2,1)S(1)} %get-tuple-element.5.row_ref), custom_call_target="tpu_custom_call" | custom-call | tf_op jit(solution)/shard_map/pallas_call | solution.py:324

commit v7 on v6

--- a/solution.py
+++ b/solution.py
@@ -64,8 +64,7 @@
     partner = lax.rem(me + 16, 32)
     xs = [cx] + [lax.rem(cx + d, 4) for d in (1, 2, 3)]
     zs = [cz] + [lax.rem(cz + d, 4) for d in (1, 2, 3)]
-    away = [(2, 2), (2, 1), (1, 2), (2, 3), (3, 2), (2, 0), (0, 2), (1, 1), (3, 3), (1, 3), (3, 1)]
-    away += [(1, 0), (0, 1), (3, 0), (0, 3)]
+    away = [(2, 2), (2, 1), (3, 2), (2, 3), (1, 2), (1, 1), (3, 3), (3, 1), (1, 3), (2, 0), (0, 2), (1, 0), (0, 3), (3, 0), (0, 1)]
     to = [(xs[dx] * 4 + zs[dz]) * 2 + core for dx, dz in away]
     source = [(xs[(4 - dx) % 4] * 4 + zs[(4 - dz) % 4]) * 2 + core for dx, dz in away]
 

time: 27.3 us -> 26.8 us (0.982)
  Pallas kernels: 26.5 us -> 26 us
    pallas_call x1, Pallas kernels: 25.8 us -> 25.2 us  [local(): pl.pallas_call(kernel, out_shape=(pltpu.VMEM((2, 128, LAT), bf16), pltpu....]
where the time goes in v7:
time: 26.8 us; the launch traced here: 26.6 us
  Pallas kernels  26 us (97%)
  between operations  0.64 us (2%)
    pallas_call x1, Pallas kernels, local(): pl.pallas_call(kernel, out_shape=(pltpu.VMEM((2, 128, LAT), bf16), pltpu....  25.2 us
    pallas_call x1, Pallas kernels, local(): pl.pallas_call(finish, out_shape=(pltpu.HBM((2, 128, LAT), bf16), pltpu.H...  0.72 us

profile of v7, /device:TPU:1, one launch (start us, length us, event | category | flops | bytes accessed | tf_op | source)
XLA Modules:
  0.0 26.6 jit_solution(16643744489852090965)
XLA Ops:
  0.6 25.2 %shard_map.113 = (bf16[2,128,512]{2,1,0:T(8,128)(2,1)S(1)}, bf16[16,512]{1,0:T(8,128)(2,1)S(1)}) custom-call(bf16[2,576,128]{2,1,0:T(8,128)(2,1)} %bitcast.3, bf16[2,576,1024]{2,1,0:T(8,128)(2,1)} %bitcast.2, s32[64]{0:T(128)} %len_hbm.1, s32[16]{0:T(128)} %trade_hbm.1, bf16[2,3584]{1,0:T(2,128)(2,1)} %tok_hbm.1, s32[2,8]{1,0:T(2,128)} %rout_hbm.1, ...), custom_call_target="tpu_custom_call" | custom-call | flops 2000000000 | bytes 25000000 | tf_op jit(solution)/shard_map/pallas_call | solution.py:251
  25.9 0.7 %shard_map.114 = (bf16[2,128,512]{2,1,0:T(8,128)(2,1)}, bf16[2,3584]{1,0:T(2,128)(2,1)}) custom-call(bf16[2,128,512]{2,1,0:T(8,128)(2,1)S(1)} %get-tuple-element.4.att_ref, bf16[16,512]{1,0:T(8,128)(2,1)S(1)} %get-tuple-element.5.row_ref), custom_call_target="tpu_custom_call" | custom-call | tf_op jit(solution)/shard_map/pallas_call | solution.py:323

commit v8 on v7

--- a/solution.py
+++ b/solution.py
@@ -198,13 +198,18 @@
             send(sums.at[other_core, cut], mate_in.at[cut], mate_s.at[i], mate_r.at[i], mate)
         )
         mate_copies[i].start()
-    for copy in mate_copies:
-        copy.wait_recv()
-    part = (sums[core].astype(f32) + mate_in[...].astype(f32)).astype(bf16)
-    part = jnp.concatenate([part.reshape(PIECES * 32, W), jnp.zeros((32, W), bf16)], axis=0)
-    back[...] = (
-        jnp.dot(perm[1], part, preferred_element_type=f32).astype(bf16).reshape(16, 16, W)
-    )
+    blocks = jnp.zeros((256, W), f32)
+    for i, (first, last) in enumerate(CUTS):
+        mate_copies[i].wait_recv()
+        cut = pl.ds(first, last - first)
+        part = (sums[core, cut].astype(f32) + mate_in[cut].astype(f32)).astype(bf16)
+        part = part.reshape((last - first) * 32, W)
+        if last == PIECES:
+            part = jnp.concatenate([part, jnp.zeros((32, W), bf16)], axis=0)
+        blocks += jnp.dot(
+            perm[1, :, first * 32 : first * 32 + 128], part, preferred_element_type=f32
+        )
+    back[...] = blocks.astype(bf16).reshape(16, 16, W)
     back_copies = [
         send(back.at[i], landed.at[i], back_s, back_r, source[i])
         for i in range(15)

time: 26.8 us -> 26.9 us (level)
  no operation moved by 1% of the time
where the time goes in v8:
time: 26.9 us; the launch traced here: 26.6 us
  Pallas kernels  26 us (97%)
  between operations  0.64 us (2%)
    pallas_call x1, Pallas kernels, local(): pl.pallas_call(kernel, out_shape=(pltpu.VMEM((2, 128, LAT), bf16), pltpu....  25.3 us
    pallas_call x1, Pallas kernels, local(): pl.pallas_call(finish, out_shape=(pltpu.HBM((2, 128, LAT), bf16), pltpu.H...  0.72 us

profile of v8, /device:TPU:1, one launch (start us, length us, event | category | flops | bytes accessed | tf_op | source)
XLA Modules:
  0.0 26.6 jit_solution(1720482627026755410)
XLA Ops:
  0.6 25.3 %shard_map.113 = (bf16[2,128,512]{2,1,0:T(8,128)(2,1)S(1)}, bf16[16,512]{1,0:T(8,128)(2,1)S(1)}) custom-call(bf16[2,576,128]{2,1,0:T(8,128)(2,1)} %bitcast.3, bf16[2,576,1024]{2,1,0:T(8,128)(2,1)} %bitcast.2, s32[64]{0:T(128)} %len_hbm.1, s32[16]{0:T(128)} %trade_hbm.1, bf16[2,3584]{1,0:T(2,128)(2,1)} %tok_hbm.1, s32[2,8]{1,0:T(2,128)} %rout_hbm.1, ...), custom_call_target="tpu_custom_call" | custom-call | flops 2000000000 | bytes 25000000 | tf_op jit(solution)/shard_map/pallas_call | solution.py:256
  25.9 0.7 %shard_map.114 = (bf16[2,128,512]{2,1,0:T(8,128)(2,1)}, bf16[2,3584]{1,0:T(2,128)(2,1)}) custom-call(bf16[2,128,512]{2,1,0:T(8,128)(2,1)S(1)} %get-tuple-element.4.att_ref, bf16[16,512]{1,0:T(8,128)(2,1)S(1)} %get-tuple-element.5.row_ref), custom_call_target="tpu_custom_call" | custom-call | tf_op jit(solution)/shard_map/pallas_call | solution.py:328
